TPU v7x, 512 devices: a whole 4x8x8 slice. The times are simulated.
512 devices in a mesh: sample: 8 (over y_hi, core), prefix: 64 (over x, y_lo, z).
Axes of the slice: x: 4, y: 8 (y_hi: 4, y_lo: 2; y = y_hi * 2 + y_lo), z: 8, core: 2. Of those that a mesh axis runs over, the one named last changes fastest.
Arguments:
- resp_q: bfloat16 [512, 128, 4096], P(('sample', 'prefix')), may hold values from -6 to 6
- resp_k: bfloat16 [512, 128, 512], P(('sample', 'prefix')), may hold values from -6 to 6
- resp_v: bfloat16 [512, 128, 512], P(('sample', 'prefix')), may hold values from -6 to 6
- resp_do: bfloat16 [512, 128, 4096], P(('sample', 'prefix')), may hold values from -6 to 6
- resp_out: bfloat16 [512, 128, 4096], P(('sample', 'prefix')), may hold values from -6 to 6
- resp_lse: float32 [512, 128, 32], P(('sample', 'prefix'))
- prompt_k: bfloat16 [1024, 512], P('prefix'), may hold values from -6 to 6
- prompt_v: bfloat16 [1024, 512], P('prefix'), may hold values from -6 to 6
- resp_lengths: int32 [512], P(('sample', 'prefix')), may hold values from 16 to 128, as said below
Outputs:
- resp_dq: bfloat16 [512, 128, 4096], P(('sample', 'prefix'))
- resp_dk: bfloat16 [512, 128, 512], P(('sample', 'prefix'))
- resp_dv: bfloat16 [512, 128, 512], P(('sample', 'prefix'))
- prompt_dk: float32 [1024, 512], P('prefix')
- prompt_dv: float32 [1024, 512], P('prefix')
Inputs may be any that keep to these rules, and one draw needn't show every extreme that they name: `resp_lengths`: some response has exactly 128 live tokens and some has 16.
All inputs are finite; a program needn't handle non-finite values.
Results may differ from a plain program's by a relative error of at most 0.0051.
Values may be sent and summed in bfloat16 or wider, within the bound.
No kernel may reach another device: no remote copies, remote signals or barrier semaphores. Data moves between devices by JAX's collectives and lax.ppermute only.
A program may use at most 64 MiB of HBM per device.

v0:
```python
import jax
import jax.numpy as jnp
from jax import lax
from jax.sharding import PartitionSpec as P

H = 32
KVH = 4
HD = 128


def block_size(total_rows):
    return max((size for size in range(1, min(total_rows, 256) + 1) if total_rows % size == 0))


def body(resp_q, resp_k, resp_v, resp_do, resp_out, resp_lse, prompt_k, prompt_v, resp_lengths):
    pair_count, row_count, _ = resp_q.shape
    groups = H // KVH
    kv_width = KVH * HD
    score_scale = HD ** (-0.5)
    shard_count = lax.axis_size("prefix")
    query_pos = jnp.arange(row_count, dtype=jnp.int32)
    live_rows = query_pos[None, :] < resp_lengths[:, None]
    query_heads = resp_q.reshape(pair_count, row_count, KVH, groups, HD)
    grad_heads = resp_do.reshape(pair_count, row_count, KVH, groups, HD)
    out_heads = resp_out.reshape(pair_count, row_count, KVH, groups, HD)
    out_dot = jnp.sum(grad_heads.astype(jnp.float32) * out_heads.astype(jnp.float32), -1)
    dot_cols = out_dot.transpose(0, 2, 3, 1)[..., None]
    lse_cols = resp_lse.reshape(pair_count, row_count, KVH, groups).transpose(0, 2, 3, 1)[..., None]

    def key_block(block_keys, block_values, live_mask, shared):
        key_form = "ukd" if shared else "bukd"
        key_heads = block_keys.reshape(block_keys.shape[:-1] + (KVH, HD))
        value_heads = block_values.reshape(block_values.shape[:-1] + (KVH, HD))
        scores = (
            jnp.einsum(
                "btkgd," + key_form + "->bkgtu",
                query_heads,
                key_heads,
                preferred_element_type=jnp.float32,
            )
            * score_scale
        )
        probs = jnp.exp(scores - lse_cols) * live_mask[:, None, None].astype(jnp.float32)
        prob_grad = jnp.einsum(
            "btkgd," + key_form + "->bkgtu",
            grad_heads,
            value_heads,
            preferred_element_type=jnp.float32,
        )
        score_grad = probs * (prob_grad - dot_cols)
        probs_low = probs.astype(jnp.bfloat16)
        score_low = score_grad.astype(jnp.bfloat16)
        query_grad = (
            jnp.einsum(
                "bkgtu," + key_form + "->btkgd",
                score_low,
                key_heads,
                preferred_element_type=jnp.float32,
            )
            * score_scale
        )
        key_grad = (
            jnp.einsum(
                "bkgtu,btkgd->" + key_form,
                score_low,
                query_heads,
                preferred_element_type=jnp.float32,
            )
            * score_scale
        )
        value_grad = jnp.einsum(
            "bkgtu,btkgd->" + key_form, probs_low, grad_heads, preferred_element_type=jnp.float32
        )
        both_grads = jnp.concatenate(
            [
                key_grad.reshape(key_grad.shape[:-2] + (kv_width,)),
                value_grad.reshape(value_grad.shape[:-2] + (kv_width,)),
            ],
            -1,
        )
        return (query_grad, both_grads)

    prompt_total = prompt_k.shape[0] * shard_count
    query_zero = jnp.zeros((pair_count, row_count, KVH, groups, HD), jnp.float32)
    prompt_zero = jnp.zeros((prompt_total, 2 * kv_width), jnp.float32)
    pieces = (
        lax.all_gather(prompt_k, "prefix", axis=0, tiled=True),
        lax.all_gather(prompt_v, "prefix", axis=0, tiled=True),
    )
    piece_rows = pieces[0].shape[0]
    prompt_size = block_size(piece_rows)
    count = piece_rows // prompt_size
    keys_split = pieces[0].reshape(count, prompt_size, kv_width)
    values_split = pieces[1].reshape(count, prompt_size, kv_width)
    live_mask = jnp.broadcast_to(live_rows[:, :, None], (pair_count, row_count, prompt_size))

    def inner(query_acc, items):
        query_grad, both_grads = key_block(items[0], items[1], live_mask, True)
        return (query_acc + query_grad, both_grads)

    query_acc, grads = lax.scan(inner, query_zero, (keys_split, values_split))
    grads = grads.reshape(piece_rows, 2 * kv_width)
    query_sum = query_acc
    prompt_terms = lax.dynamic_update_slice_in_dim(prompt_zero, grads, jnp.int32(0), 0)
    size = block_size(row_count)
    count = row_count // size
    keys_split = resp_k.reshape(pair_count, count, size, kv_width).transpose(1, 0, 2, 3)
    values_split = resp_v.reshape(pair_count, count, size, kv_width).transpose(1, 0, 2, 3)
    block_index = jnp.arange(count, dtype=jnp.int32)

    def own_step(query_acc, items):
        key_pos = items[2] * size + jnp.arange(size, dtype=jnp.int32)
        live_mask = (key_pos[None, None, :] <= query_pos[None, :, None]) & live_rows[:, :, None]
        query_grad, both_grads = key_block(items[0], items[1], live_mask, False)
        return (query_acc + query_grad, both_grads)

    query_sum, own_terms = lax.scan(own_step, query_sum, (keys_split, values_split, block_index))
    own_grads = own_terms.transpose(1, 0, 2, 3).reshape(pair_count, row_count, 2 * kv_width)
    resp_dq = query_sum.reshape(pair_count, row_count, H * HD).astype(jnp.bfloat16)
    resp_dk = own_grads[..., :kv_width].astype(jnp.bfloat16)
    resp_dv = own_grads[..., kv_width:].astype(jnp.bfloat16)
    local_sum = lax.psum_scatter(prompt_terms, "prefix", scatter_dimension=0, tiled=True)
    prompt_grads = lax.psum(local_sum, "sample")
    return (resp_dq, resp_dk, resp_dv, prompt_grads[:, :kv_width], prompt_grads[:, kv_width:])


def solution(mesh):
    return jax.shard_map(
        body,
        mesh=mesh,
        in_specs=(
            P(("sample", "prefix"), None, None),
            P(("sample", "prefix"), None, None),
            P(("sample", "prefix"), None, None),
            P(("sample", "prefix"), None, None),
            P(("sample", "prefix"), None, None),
            P(("sample", "prefix"), None, None),
            P("prefix", None),
            P("prefix", None),
            P(("sample", "prefix")),
        ),
        out_specs=(
            P(("sample", "prefix"), None, None),
            P(("sample", "prefix"), None, None),
            P(("sample", "prefix"), None, None),
            P("prefix", None),
            P("prefix", None),
        ),
        check_vma=False,
    )
```

profile of v0, /device:TPU:1, one launch (start us, length us, event | category | flops | bytes accessed | tf_op | source)
XLA Modules:
  0.0 1083.4 jit_solution(6693617847802084570)
XLA Ops:
  8.7 1.6 copy.68
  10.4 1.3 copy.69
  11.7 1.5 copy.70
  13.8 1.5 multiply_reduce_fusion
  15.4 257.0 %all-gather.3.cloned.1.call-done = bf16[1024,512]{1,0:T(8,128)(2,1)} async-done(((bf16[16,512]{1,0:T(8,128)(2,1)}), bf16[1024,512]{1,0:T(8,128)(2,1)}) %all-gather.3.cloned.1.call-update) | async-done | bytes 1048592 | tf_op jit(solution)/shard_map/all_gather | solution.py:87
  272.4 298.7 %all-gather.5.cloned.1.call-done = bf16[1024,512]{1,0:T(8,128)(2,1)} async-done(((bf16[16,512]{1,0:T(8,128)(2,1)}), bf16[1024,512]{1,0:T(8,128)(2,1)}) %all-gather.5.cloned.1.call-update) | async-done | bytes 1048592 | tf_op jit(solution)/shard_map/all_gather | solution.py:88
  571.0 67.1 %while.3 = (s32[]{:T(128)}, f32[1,128,4,8,128]{1,4,3,2,0:T(8,128)}, f32[4,256,1024]{2,1,0:T(8,128)}, bf16[4,256,512]{2,1,0:T(8,128)(2,1)}, bf16[1,128,4,8,128]{1...) while((s32[]{:T(128)}, ...), condition=%wide.region_2.3_spmd.clone, body=%wide.region_1.2_spmd.clone.sunk | while | flops 1354629248 | bytes 54314796 | solution.py:101
  571.0 1.1 constant_dynamic-slice_fusion.3
  572.2 2.7 fusion.81
  574.9 0.8 copy.128
  575.8 3.9 fusion.82
  579.7 1.9 bitcast_add_fusion.3
  581.7 1.0 copy-done
  582.7 2.3 fusion.83
  585.0 0.8 fusion.84
  586.2 1.0 constant_dynamic-update-slice_fusion.2
  587.2 1.1 constant_dynamic-slice_fusion.3
  588.4 2.7 fusion.81
  591.1 0.8 copy.128
  592.0 3.9 fusion.82
  595.9 3.7 bitcast_add_fusion.3
  599.6 2.3 fusion.83
  601.9 0.8 fusion.84
  603.1 1.1 constant_dynamic-update-slice_fusion.2
  604.2 1.1 constant_dynamic-slice_fusion.3
  605.4 2.7 fusion.81
  608.1 0.8 copy.128
  609.0 3.9 fusion.82
  612.9 3.7 bitcast_add_fusion.3
  616.6 2.3 fusion.83
  618.9 0.8 fusion.84
  620.1 1.1 constant_dynamic-update-slice_fusion.2
  621.2 1.1 constant_dynamic-slice_fusion.3
  622.4 2.7 fusion.81
  625.1 0.8 copy.128
  625.9 3.9 fusion.82
  629.9 3.7 bitcast_add_fusion.3
  633.6 2.3 fusion.83
  635.9 0.8 fusion.84
  637.1 1.1 constant_dynamic-update-slice_fusion.2
  638.3 0.8 copy-done.7
  639.9 2.4 fusion.36
  644.1 2.5 fusion.39
  647.4 308.4 %reduce-scatter.2.cloned.1.call-done = f32[16,1024]{1,0:T(8,128)} async-done(((f32[1024,1024]{1,0:T(8,128)}), f32[16,1024]{1,0:T(8,128)}) %reduce-scatter.2.cloned.1.call-update) | async-done | bytes 65552 | tf_op jit(solution)/shard_map/reduce_scatter | solution.py:122
  955.9 1.4 fusion.31
  957.3 2.3 copy.84
  959.6 116.0 %all-reduce.2.cloned.1.call-done = f32[16,1024]{1,0:T(8,128)} async-done(((f32[16,1024]{1,0:T(8,128)}), f32[16,1024]{1,0:T(8,128)}) %all-reduce.2.cloned.1.call-update) | async-done | bytes 65552 | tf_op jit(solution)/shard_map/psum | solution.py:123
  1075.5 1.4 fusion.45
  (57 shorter events, 7.1 us)
Async XLA Ops:
  7.2 3.2 copy-start.5
  7.2 265.2 %all-gather.3.cloned.1.call-start = ((), (), s32[]{:S(2)}) async-start(), calls=%async_computation.1 | async-start | bytes 1064960 | tf_op jit(solution)/shard_map/all_gather | solution.py:87
  7.9 563.1 %all-gather.5.cloned.1.call-start = ((), (), s32[]{:S(2)}) async-start(), calls=%async_computation.2 | async-start | bytes 1064960 | tf_op jit(solution)/shard_map/all_gather | solution.py:88
  8.7 947.2 %reduce-scatter.2.cloned.1.call-start = ((), (), s32[]{:S(2)}) async-start(), calls=%async_computation.3 | async-start | bytes 4259840 | tf_op jit(solution)/shard_map/reduce_scatter | solution.py:122
  13.2 557.9 %copy-start.6 = (f32[1,128,32]{1,2,0:T(8,128)S(1)}, f32[1,128,32]{1,2,0:T(8,128)}, u32[]{:S(2)}) copy-start(f32[1,128,32]{1,2,0:T(8,128)} %param.16) | copy-start | bytes 49156
  579.7 2.9 copy-start
  595.9 3.7 copy-start
  612.9 3.7 copy-start
  629.9 3.7 copy-start
  638.2 0.9 copy-start.7
  638.2 1.1 copy-start.8
  638.2 437.3 %all-reduce.2.cloned.1.call-start = ((), (), s32[]{:S(2)}) async-start(), calls=%async_computation.4 | async-start | bytes 131072 | tf_op jit(solution)/shard_map/psum | solution.py:123
  639.9 2.4 copy-start.2
  642.4 1.0 copy-start.3
  643.3 312.5 %copy-start.1 = (f32[1,128,4,8,128]{1,4,3,2,0:T(8,128)S(1)}, f32[1,128,4,8,128]{1,4,3,2,0:T(8,128)}, u32[]{:S(2)}) copy-start(f32[1,128,4,8,128]{1,4,3,2,0:T(8,128)} %get-tuple-element.91) | copy-start | bytes 6291460
  643.3 312.5 %copy-start.4 = (bf16[4,8,128,128]{2,3,1,0:T(8,128)(2,1)S(1)}, bf16[4,8,128,128]{2,3,1,0:T(8,128)(2,1)}, u32[]{:S(2)}) copy-start(bf16[4,8,128,128]{2,3,1,0:T(8,128)(2,1)} %copy-done.3) | copy-start | bytes 3145732
Sparse Core Ops, SparseCore 0:
  10.1 262.2 all-gather.2
  274.5 296.5 all-gather.4
  638.3 317.4 reduce-scatter.1
  958.8 116.6 all-reduce.1
where the time goes:
time: 1080 us
  waiting for transfers between devices  981 us (91%)
  matrix products  59.1 us (5%)
  local copies, waits for them, and re-layouts  26 us (2%)
  between operations  14.6 us (1%)
    reduce_scatter x1, waiting for transfers between devices, body(): lax.psum_scatter(prompt_terms, 'prefix', scatter_dimension=0, tiled=True)  308 us
    all_gather x1, waiting for transfers between devices, body(): lax.all_gather(prompt_v, 'prefix', axis=0, tiled=True)  299 us
    all_gather x1, waiting for transfers between devices, body(): lax.all_gather(prompt_k, 'prefix', axis=0, tiled=True)  257 us
    psum x1, waiting for transfers between devices, body(): prompt_grads = lax.psum(local_sum, 'sample')  116 us
  transfers between devices with their start and end apart: 4, of which 4 were waited for; matrix products, arithmetic and copies ran while one was open for 2% of the time, Pallas kernels for 0%

commit v1 on v0

v1 whole, which is shorter than its diff:
```python
import functools
import math

import jax
import jax.numpy as jnp
from jax import lax
from jax.experimental import pallas as pl
from jax.experimental.pallas import tpu as pltpu
from jax.sharding import Mesh
from jax.sharding import PartitionSpec as P

H = 32
KVH = 4
HD = 128
R = 128
G = H // KVH
QR = G * R
SCALE = HD**-0.5
LOG2E = math.log2(math.e)
AXES = ("yh", "core", "x", "yl", "zh", "zl")
f32 = jnp.float32
bf16 = jnp.bfloat16

OFF_DO = QR
OFF_K = 2 * QR
OFF_V = OFF_K + R
OFF_ST = OFF_V + R
PACK = OFF_ST + 6 * G

NT = (((1,), (1,)), ((), ()))
NN = (((1,), (0,)), ((), ()))
VMEM = pl.BlockSpec(memory_space=pltpu.VMEM)
CHUNK = 512


def dot(a, b, dims):
    return lax.dot_general(a, b, dims, preferred_element_type=f32)


def split3(value):
    hi = value.astype(bf16)
    rest = value - hi.astype(f32)
    mid = rest.astype(bf16)
    low = (rest - mid.astype(f32)).astype(bf16)
    return hi, mid, low


def prep_kernel(info, q, do, out, k, v, lse, send, mine):
    step = pl.program_id(0)
    length = info[1]

    def fill(ref):
        ones = jnp.ones((8, HD), bf16)
        rows = []
        for h in range(G):
            cols = slice(h * HD, (h + 1) * HD)
            rs = slice(h * R, (h + 1) * R)
            ref[0, rs, :] = q[:, cols]
            dh = do[:, cols]
            ref[0, OFF_DO + h * R : OFF_DO + (h + 1) * R, :] = dh
            prod = dh.astype(f32) * out[:, cols].astype(f32)
            hi = prod.astype(bf16)
            low = (prod - hi.astype(f32)).astype(bf16)
            rows.append((dot(ones, hi, NT) + dot(ones, low, NT))[0:1, :])
        ref[0, OFF_K : OFF_K + R, :] = k[...]
        ref[0, OFF_V : OFF_V + R, :] = v[...]
        delta = jnp.concatenate(rows, 0)
        token = lax.broadcasted_iota(jnp.int32, (G, R), 1)
        lse2 = jnp.where(token < length, lse[...] * LOG2E, 1e30)
        ref[0, OFF_ST:PACK, :] = jnp.concatenate(split3(lse2) + split3(delta), 0)

    @pl.when(step < 2)
    def _():
        fill(send)

    @pl.when(step >= 2)
    def _():
        fill(mine)


def prep(core, length, q, do, out, k, v, lse_t):
    def head(i, info):
        return jnp.where(i < 2, 2 * (1 - info[0]) + i, 2 * info[0] + i - 2)

    wide = pl.BlockSpec((R, QR), lambda i, info: (0, head(i, info)))
    narrow = pl.BlockSpec((R, HD), lambda i, info: (0, head(i, info)))
    shape = jax.ShapeDtypeStruct((2, PACK, HD), bf16)
    return pl.pallas_call(
        prep_kernel,
        out_shape=(shape, shape),
        grid_spec=pltpu.PrefetchScalarGridSpec(
            num_scalar_prefetch=1,
            grid=(4,),
            in_specs=[wide, wide, wide, narrow, narrow, pl.BlockSpec((G, R), lambda i, info: (head(i, info), 0))],
            out_specs=(
                pl.BlockSpec((1, PACK, HD), lambda i, info: (jnp.minimum(i, 1), 0, 0)),
                pl.BlockSpec((1, PACK, HD), lambda i, info: (jnp.maximum(i - 2, 0), 0, 0)),
            ),
        ),
        compiler_params=pltpu.CompilerParams(vmem_limit_bytes=20 * 2**20),
        cost_estimate=pl.CostEstimate(flops=10**7, bytes_accessed=6 * 2**20, transcendentals=0),
        name="prep",
    )(jnp.stack([core, length]), q, do, out, k, v, lse_t)


def stat_row(ref, g, kind, first, count):
    base = OFF_ST + kind * 3 * G
    block = [ref[g, base + term * G : base + (term + 1) * G, :].astype(f32) for term in range(3)]
    total = block[0] + block[1] + block[2]
    return jnp.concatenate([total[h : h + 1, :] for h in range(first, first + count)], 1)


def tile_grads(ref, g, chunk, keys, values, causal):
    cs = slice(chunk * CHUNK, (chunk + 1) * CHUNK)
    qc = ref[g, cs, :]
    dc = ref[g, OFF_DO + chunk * CHUNK : OFF_DO + (chunk + 1) * CHUNK, :]
    heads = CHUNK // R
    lse2 = stat_row(ref, g, 0, chunk * heads, heads)
    delta = stat_row(ref, g, 1, chunk * heads, heads)
    scores = dot(keys, qc, NT)
    prob_grad = dot(values, dc, NT)
    probs = jnp.exp2(scores * (SCALE * LOG2E) - lse2)
    if causal:
        shape = scores.shape
        token = lax.broadcasted_iota(jnp.int32, shape, 1) % R
        probs = jnp.where(lax.broadcasted_iota(jnp.int32, shape, 0) <= token, probs, 0.0)
    score_low = (probs * (prob_grad - delta)).astype(bf16)
    dv = dot(probs.astype(bf16), dc, NN)
    dk = dot(score_low, qc, NN)
    dq = lax.dot_general(keys, score_low, (((0,), (0,)), ((), ())), preferred_element_type=f32).T
    return dk, dv, dq, cs


def own_kernel(mine, recv, dq, grads):
    for r, ref in enumerate((mine, recv)):
        for g in range(2):
            keys = ref[g, OFF_K : OFF_K + R, :]
            values = ref[g, OFF_V : OFF_V + R, :]
            dk = jnp.zeros((R, HD), f32)
            dv = jnp.zeros((R, HD), f32)
            for chunk in range(QR // CHUNK):
                dk_c, dv_c, dq_c, cs = tile_grads(ref, g, chunk, keys, values, True)
                dk += dk_c
                dv += dv_c
                dq[r, g, cs, :] = dq_c
            grads[r, :, g * HD : (g + 1) * HD] = (dk * SCALE).astype(bf16)
            grads[r, :, (2 + g) * HD : (3 + g) * HD] = dv.astype(bf16)


def prompt_block(mine, recv, kv, emit_dq, out):
    for g in range(2):
        keys = kv[:, g * HD : (g + 1) * HD]
        values = kv[:, (2 + g) * HD : (3 + g) * HD]
        rows = kv.shape[0]
        dk = jnp.zeros((rows, HD), f32)
        dv = jnp.zeros((rows, HD), f32)
        for r, ref in enumerate((mine, recv)):
            for chunk in range(QR // CHUNK):
                dk_c, dv_c, dq_c, cs = tile_grads(ref, g, chunk, keys, values, False)
                dk += dk_c
                dv += dv_c
                emit_dq(r, g, chunk, cs, dq_c)
        out[:, g * HD : (g + 1) * HD] = (dk * SCALE).astype(out.dtype)
        out[:, (2 + g) * HD : (3 + g) * HD] = dv.astype(out.dtype)


def block_kernel(mine, recv, kv, dq_in, dq, out):
    def emit_dq(r, g, chunk, cs, value):
        dq[r, g, cs, :] = dq_in[r, g, cs, :] + value

    prompt_block(mine, recv, kv, emit_dq, out)


def last_kernel(mine, recv, kv, dq_in, grads, own, back, out):
    def emit_dq(r, g, chunk, cs, value):
        total = ((dq_in[r, g, cs, :] + value) * SCALE).astype(bf16)
        target = own if r == 0 else back
        for j in range(CHUNK // R):
            h = g * G + chunk * (CHUNK // R) + j
            target[:, h * HD : (h + 1) * HD] = total[j * R : (j + 1) * R, :]

    prompt_block(mine, recv, kv, emit_dq, out)
    back[:, 2 * QR :] = grads[1]


def cost(rows):
    return pl.CostEstimate(
        flops=5 * 2 * rows * 4 * QR * HD, bytes_accessed=8 * 2**20, transcendentals=rows * 4 * QR
    )


PARAMS = pltpu.CompilerParams(vmem_limit_bytes=24 * 2**20)


def body(resp_q, resp_k, resp_v, resp_do, resp_out, resp_lse, prompt_k, prompt_v, resp_lengths):
    core = lax.axis_index("core").astype(jnp.int32)
    rows = prompt_k.shape[0]
    half = 2 * HD

    send, mine = prep(
        core, resp_lengths[0], resp_q[0], resp_do[0], resp_out[0], resp_k[0], resp_v[0], resp_lse[0].T
    )
    recv = lax.ppermute(send, "core", [(0, 1), (1, 0)])

    shard = jnp.concatenate(
        [
            lax.dynamic_slice_in_dim(prompt_k, core * half, half, 1),
            lax.dynamic_slice_in_dim(prompt_v, core * half, half, 1),
        ],
        1,
    )
    inner = ("yl", "zh", "zl")
    kv0 = lax.all_to_all(jnp.tile(shard, (16, 1)), inner, 0, 0, tiled=True)

    def along_x(value, shift):
        return lax.ppermute(value, "x", [(i, (i + shift) % 4) for i in range(4)])

    block_rows = 16 * rows
    blocks = {shift: along_x(kv0, -shift) for shift in (1, 3, 2)}
    dq_shape = jax.ShapeDtypeStruct((2, 2, QR, HD), f32)
    part_shape = jax.ShapeDtypeStruct((block_rows, 4 * HD), bf16)
    dq, grads = pl.pallas_call(
        own_kernel,
        out_shape=(dq_shape, jax.ShapeDtypeStruct((2, R, 4 * HD), bf16)),
        in_specs=[VMEM] * 2,
        out_specs=(VMEM,) * 2,
        compiler_params=PARAMS,
        cost_estimate=cost(R),
        name="own_keys",
    )(mine, recv)
    parts = []
    for shift in (1, 3, 2):
        dq, part = pl.pallas_call(
            block_kernel,
            out_shape=(dq_shape, part_shape),
            in_specs=[VMEM] * 4,
            out_specs=(VMEM,) * 2,
            input_output_aliases={3: 0},
            compiler_params=PARAMS,
            cost_estimate=cost(block_rows),
            name="prompt_block",
        )(mine, recv, blocks[shift], dq)
        parts.append(along_x(part, shift))
    own_dq, back, part0 = pl.pallas_call(
        last_kernel,
        out_shape=(
            jax.ShapeDtypeStruct((R, 2 * QR), bf16),
            jax.ShapeDtypeStruct((R, 2 * QR + 4 * HD), bf16),
            jax.ShapeDtypeStruct((block_rows, 4 * HD), f32),
        ),
        in_specs=[VMEM] * 5,
        out_specs=(VMEM,) * 3,
        compiler_params=PARAMS,
        cost_estimate=cost(block_rows),
        name="prompt_last",
    )(mine, recv, kv0, dq, grads)
    got = lax.ppermute(back, "core", [(0, 1), (1, 0)])

    total = (part0 + (parts[0].astype(f32) + parts[1].astype(f32)) + parts[2].astype(f32)).astype(bf16)
    total = lax.all_to_all(total, inner, 0, 0, tiled=True)
    total = jnp.sum(total.reshape(16, rows, 4 * HD).astype(f32), 0).astype(bf16)
    total = lax.all_to_all(jnp.tile(total, (8, 1)), ("yh", "core"), 0, 0, tiled=True)
    total = jnp.sum(total.reshape(4, 2, rows, 2, 2, HD).astype(f32), 0)
    prompt_dk = total[:, :, 0].transpose(1, 0, 2, 3).reshape(rows, KVH * HD)
    prompt_dv = total[:, :, 1].transpose(1, 0, 2, 3).reshape(rows, KVH * HD)

    def join(first, second):
        return jnp.where(
            core == 0, jnp.concatenate([first, second], -1), jnp.concatenate([second, first], -1)
        )[None]

    resp_dq = join(own_dq, got[:, : 2 * QR])
    resp_dk = join(grads[0][:, :half], got[:, 2 * QR : 2 * QR + half])
    resp_dv = join(grads[0][:, half:], got[:, 2 * QR + half :])
    return resp_dq, resp_dk, resp_dv, prompt_dk, prompt_dv


def solution(mesh):
    fine = Mesh(mesh.devices.reshape(4, 2, 4, 2, 4, 2), AXES)
    both = P(AXES, None, None)
    prefix = P(("x", "yl", "zh", "zl"), None)
    return jax.shard_map(
        body,
        mesh=fine,
        in_specs=(both,) * 6 + (prefix, prefix, P(AXES)),
        out_specs=(both, both, both, prefix, prefix),
        check_vma=False,
    )
```

time: 1080 us -> 113 us (0.10)
  waiting for transfers between devices: 981 us -> 13 us
  matrix products: 59.1 us -> 0 us
  starting transfers between devices: 0.16 us -> 50.5 us
  Pallas kernels: 0 us -> 20.9 us
  local copies, waits for them, and re-layouts: 26 us -> 8.48 us
  blocking collectives: 0 us -> 14.1 us
  between operations: 14.6 us -> 1.59 us
    all_gather x2 -> x0, waiting for transfers between devices: 556 us -> none  [the longest x1 299 us: body(): lax.all_gather(prompt_v, 'prefix', axis=0, tiled=True)]
    reduce_scatter x1 -> x0, waiting for transfers between devices: 308 us -> none  [body(): lax.psum_scatter(prompt_terms, 'prefix', scatter_dimension=0, tiled=True)]
    psum x1 -> x0, waiting for transfers between devices: 116 us -> none  [body(): prompt_grads = lax.psum(local_sum, 'sample')]
    dot_general x25 -> x0, matrix products: 59.1 us -> none  [the longest x5 18.1 us: key_block(): jnp.einsum('btkgd,' + key_form + '->bkgtu', grad_heads, value_heads, pref...]
    ppermute x0 -> x8, starting transfers between devices: none -> 34.9 us  [the longest x6 19.8 us: along_x(): return lax.ppermute(value, 'x', [(i, (i + shift) % 4) for i in range(4)])]
    pallas_call x0 -> x6, Pallas kernels: none -> 20.9 us  [the longest x3 10.5 us: body(): pl.pallas_call(block_kernel, out_shape=(dq_shape, part_shape), in_specs=[...]
    all_to_all x0 -> x2, starting transfers between devices: none -> 15.6 us  [the longest x1 9.74 us: body(): lax.all_to_all(jnp.tile(total, (8, 1)), ('yh', 'core'), 0, 0, tiled=True)]
    all_to_all x0 -> x1, blocking collectives: none -> 14.1 us  [body(): kv0 = lax.all_to_all(jnp.tile(shard, (16, 1)), inner, 0, 0, tiled=True)]
  transfers between devices with their start and end apart: 4 -> 10, of which waited for: 4 -> 2; matrix products, arithmetic and copies ran while one was open for 2% -> 3% of each run, Pallas kernels for 0% -> 12%
where the time goes in v1:
time: 113 us; the launch traced here: 112 us
  starting transfers between devices  50.5 us (45%)
  Pallas kernels  20.9 us (18%)
  blocking collectives  14.1 us (12%)
  waiting for transfers between devices  13 us (12%)
  local copies, waits for them, and re-layouts  8.48 us (8%)
  other arithmetic  3.67 us (3%)
  between operations  1.59 us (1%)
    ppermute x6, starting transfers between devices, along_x(): return lax.ppermute(value, 'x', [(i, (i + shift) % 4) for i in range(4)])  19.8 us
    all_to_all x1, blocking collectives, body(): kv0 = lax.all_to_all(jnp.tile(shard, (16, 1)), inner, 0, 0, tiled=True)  14.1 us
    pallas_call x3, Pallas kernels, body(): pl.pallas_call(block_kernel, out_shape=(dq_shape, part_shape), in_specs=[...  10.5 us
    all_to_all x1, starting transfers between devices, body(): lax.all_to_all(jnp.tile(total, (8, 1)), ('yh', 'core'), 0, 0, tiled=True)  9.74 us
    ppermute x1, starting transfers between devices, body(): recv = lax.ppermute(send, 'core', [(0, 1), (1, 0)])  8.77 us
    all_to_all x1, waiting for transfers between devices, body(): lax.all_to_all(jnp.tile(total, (8, 1)), ('yh', 'core'), 0, 0, tiled=True)  6.67 us
    all_to_all x1, waiting for transfers between devices, body(): total = lax.all_to_all(total, inner, 0, 0, tiled=True)  6.36 us
    ppermute x1, starting transfers between devices, body(): got = lax.ppermute(back, 'core', [(0, 1), (1, 0)])  6.33 us
  transfers between devices with their start and end apart: 10, of which 2 were waited for; matrix products, arithmetic and copies ran while one was open for 3% of the time, Pallas kernels for 12%

profile of v1, /device:TPU:1, one launch (start us, length us, event | category | flops | bytes accessed | tf_op | source)
XLA Modules:
  0.0 112.2 jit_solution(18073067970478960414)
XLA Ops:
  0.6 0.0 copy-start.6
  1.3 0.1 pad_add_fusion.info
  1.4 0.0 copy-start
  1.4 1.2 %copy-done = bf16[1,128,4096]{2,1,0:T(8,128)(2,1)S(1)} copy-done((bf16[1,128,4096]{2,1,0:T(8,128)(2,1)S(1)}, bf16[1,128,4096]{2,1,0:T(8,128)(2,1)}, u32[]{:S(2)}) %copy-start) | copy-done | bytes 1048600
  2.6 0.0 copy-start.1
  2.6 1.2 %copy-done.1 = bf16[1,128,4096]{2,1,0:T(8,128)(2,1)S(1)} copy-done((bf16[1,128,4096]{2,1,0:T(8,128)(2,1)S(1)}, bf16[1,128,4096]{2,1,0:T(8,128)(2,1)}, u32[]{:S(2)}) %copy-start.1) | copy-done | bytes 1048600
  3.8 1.2 %copy-done.2 = bf16[1,128,4096]{2,1,0:T(8,128)(2,1)S(1)} copy-done((bf16[1,128,4096]{2,1,0:T(8,128)(2,1)S(1)}, bf16[1,128,4096]{2,1,0:T(8,128)(2,1)}, u32[]{:S(2)}) %copy-start.2) | copy-done | bytes 1048600
  5.1 0.9 copy-done.3
  6.0 0.9 copy-done.4
  6.9 0.7 copy-done.5
  7.6 3.9 %prep.1 = (bf16[2,2352,128]{2,1,0:T(8,128)(2,1)}, bf16[2,2352,128]{2,1,0:T(8,128)(2,1)S(1)}) custom-call(s32[2]{0:T(128)S(1)} %pad_add_fusion.info, bf16[128,4096]{1,0:T(8,128)(2,1)S(1)} %bitcast.38, bf16[128,4096]{1,0:T(8,128)(2,1)S(1)} %bitcast.39, bf16[128,4096]{1,0:T(8,128)(2,1)S(1)} %bitcast.40, bf16[128,512]{1,0:T(8,128)(2,1)S(1)} %bitcast.42, ...), custom_call_target="tpu_custom_call" | custom-call | flops 10000000 | bytes 6291456 | tf_op jit(solution)/shard_map/prep/pallas_call | solution.py:88
  11.5 8.8 %collective-permute-start = (bf16[2,2352,128]{2,1,0:T(8,128)(2,1)}, bf16[2,2352,128]{2,1,0:T(8,128)(2,1)S(1)}, u32[]{:S(2)}, u32[]{:S(2)}) collective-permute-start(bf16[2,2352,128]{2,1,0:T(8,128)(2,1)} %get-tuple-element.19), channel_id=1, source_target_pairs={{0,64},{64,0},{1,65},{65,1},{2,66},{66,2},{3,67},{67,3},{4,68},{68... | collective-permute-start | bytes 3612680 | tf_op jit(solution)/shard_map/ppermute | solution.py:203
  20.3 0.0 copy-done.6
  20.3 0.0 copy-done.7
  20.3 14.1 %all_to_all.23 = bf16[16,16,512]{2,1,0:T(8,128)(2,1)S(1)} all-to-all(bf16[16,16,512]{2,1,0:T(8,128)(2,1)S(1)} %tile.4), channel_id=1, replica_groups=mesh['yh'=4,'core'=2,'x'=4,'yl'=2,'zh'=4,'zl'=2] {'yl','zh','zl'}, dimensions={0} | all-to-all | bytes 524288 | tf_op jit(solution)/shard_map/all_to_all | solution.py:213
  34.4 4.4 %collective-permute-start.3 = (bf16[256,512]{1,0:T(8,128)(2,1)S(1)}, bf16[256,512]{1,0:T(8,128)(2,1)S(1)}, u32[]{:S(2)}, u32[]{:S(2)}) collective-permute-start(bf16[256,512]{1,0:T(8,128)(2,1)S(1)} %bitcast.34), channel_id=1, source_target_pairs={{0,48},{16,0},{32,16},{48,32},{1,49},{17,1},{33,17},{49,33},{2,50}... | collective-permute-start | bytes 786440 | tf_op jit(solution)/shard_map/ppermute | solution.py:216
  38.8 1.9 %collective-permute-start.2 = (bf16[256,512]{1,0:T(8,128)(2,1)S(1)}, bf16[256,512]{1,0:T(8,128)(2,1)S(1)}, u32[]{:S(2)}, u32[]{:S(2)}) collective-permute-start(bf16[256,512]{1,0:T(8,128)(2,1)S(1)} %bitcast.35), channel_id=1, source_target_pairs={{0,16},{16,32},{32,48},{48,0},{1,17},{17,33},{33,49},{49,1},{2,18}... | collective-permute-start | bytes 786440 | tf_op jit(solution)/shard_map/ppermute | solution.py:216
  40.7 3.6 %collective-permute-start.1 = (bf16[256,512]{1,0:T(8,128)(2,1)S(1)}, bf16[256,512]{1,0:T(8,128)(2,1)S(1)}, u32[]{:S(2)}, u32[]{:S(2)}) collective-permute-start(bf16[256,512]{1,0:T(8,128)(2,1)S(1)} %bitcast.36), channel_id=1, source_target_pairs={{0,32},{16,48},{32,0},{48,16},{1,33},{17,49},{33,1},{49,17},{2,34}... | collective-permute-start | bytes 786440 | tf_op jit(solution)/shard_map/ppermute | solution.py:216
  44.4 0.0 collective-permute-done.recv
  44.4 2.6 %own_keys.1 = (f32[2,2,1024,128]{3,2,1,0:T(8,128)S(1)}, bf16[2,128,512]{2,1,0:T(8,128)(2,1)S(1)}) custom-call(bf16[2,2352,128]{2,1,0:T(8,128)(2,1)S(1)} %get-tuple-element.18.mine, bf16[2,2352,128]{2,1,0:T(8,128)(2,1)S(1)} %collective-permute-done.recv), custom_call_target="tpu_custom_call" | custom-call | flops 671088640 | bytes 8388608 | tf_op jit(solution)/shard_map/own_keys/pallas_call | solution.py:222
  47.0 0.0 collective-permute-done.3.kv
  47.0 3.5 %prompt_block.3 = (f32[2,2,1024,128]{3,2,1,0:T(8,128)S(1)}, bf16[256,512]{1,0:T(8,128)(2,1)S(1)}) custom-call(bf16[2,2352,128]{2,1,0:T(8,128)(2,1)S(1)} %get-tuple-element.18.mine, bf16[2,2352,128]{2,1,0:T(8,128)(2,1)S(1)} %collective-permute-done.recv, bf16[256,512]{1,0:T(8,128)(2,1)S(1)} %collective-permute-done.3.kv, ...), custom_call_target="tpu_custom_call", output_to_operand_aliasing={{0}: (3, {})} | custom-call | flops 1342177280 | bytes 8388608 | tf_op jit(solution)/shard_map/prompt_block/pallas_call | solution.py:233
  50.5 0.0 collective-permute-done.2.kv
  50.5 3.5 %prompt_block.4 = (f32[2,2,1024,128]{3,2,1,0:T(8,128)S(1)}, bf16[256,512]{1,0:T(8,128)(2,1)S(1)}) custom-call(bf16[2,2352,128]{2,1,0:T(8,128)(2,1)S(1)} %get-tuple-element.18.mine, bf16[2,2352,128]{2,1,0:T(8,128)(2,1)S(1)} %collective-permute-done.recv, bf16[256,512]{1,0:T(8,128)(2,1)S(1)} %collective-permute-done.2.kv, ...), custom_call_target="tpu_custom_call", output_to_operand_aliasing={{0}: (3, {})} | custom-call | flops 1342177280 | bytes 8388608 | tf_op jit(solution)/shard_map/prompt_block/pallas_call | solution.py:233
  54.0 0.0 collective-permute-done.1.kv
  54.0 3.5 %prompt_block.5 = (f32[2,2,1024,128]{3,2,1,0:T(8,128)S(1)}, bf16[256,512]{1,0:T(8,128)(2,1)S(1)}) custom-call(bf16[2,2352,128]{2,1,0:T(8,128)(2,1)S(1)} %get-tuple-element.18.mine, bf16[2,2352,128]{2,1,0:T(8,128)(2,1)S(1)} %collective-permute-done.recv, bf16[256,512]{1,0:T(8,128)(2,1)S(1)} %collective-permute-done.1.kv, ...), custom_call_target="tpu_custom_call", output_to_operand_aliasing={{0}: (3, {})} | custom-call | flops 1342177280 | bytes 8388608 | tf_op jit(solution)/shard_map/prompt_block/pallas_call | solution.py:233
  57.5 3.2 %collective-permute-start.7 = (bf16[256,512]{1,0:T(8,128)(2,1)S(1)}, bf16[256,512]{1,0:T(8,128)(2,1)S(1)}, u32[]{:S(2)}, u32[]{:S(2)}) collective-permute-start(bf16[256,512]{1,0:T(8,128)(2,1)S(1)} %get-tuple-element.30), channel_id=1, source_target_pairs={{0,32},{16,48},{32,0},{48,16},{1,33},{17,49},{33,1},{49,17},{2,34}... | collective-permute-start | bytes 786440 | tf_op jit(solution)/shard_map/ppermute | solution.py:216
  60.7 4.6 %collective-permute-start.6 = (bf16[256,512]{1,0:T(8,128)(2,1)S(1)}, bf16[256,512]{1,0:T(8,128)(2,1)S(1)}, u32[]{:S(2)}, u32[]{:S(2)}) collective-permute-start(bf16[256,512]{1,0:T(8,128)(2,1)S(1)} %get-tuple-element.29), channel_id=1, source_target_pairs={{0,48},{16,0},{32,16},{48,32},{1,49},{17,1},{33,17},{49,33},{2,50}... | collective-permute-start | bytes 786440 | tf_op jit(solution)/shard_map/ppermute | solution.py:216
  65.3 2.1 %collective-permute-start.5 = (bf16[256,512]{1,0:T(8,128)(2,1)S(1)}, bf16[256,512]{1,0:T(8,128)(2,1)S(1)}, u32[]{:S(2)}, u32[]{:S(2)}) collective-permute-start(bf16[256,512]{1,0:T(8,128)(2,1)S(1)} %get-tuple-element.28), channel_id=1, source_target_pairs={{0,16},{16,32},{32,48},{48,0},{1,17},{17,33},{33,49},{49,1},{2,18}... | collective-permute-start | bytes 786440 | tf_op jit(solution)/shard_map/ppermute | solution.py:216
  67.4 3.9 %prompt_last.1 = (bf16[128,2048]{1,0:T(8,128)(2,1)S(1)}, bf16[128,2560]{1,0:T(8,128)(2,1)}, f32[256,512]{1,0:T(8,128)S(1)}) custom-call(bf16[2,2352,128]{2,1,0:T(8,128)(2,1)S(1)} %get-tuple-element.18.mine, bf16[2,2352,128]{2,1,0:T(8,128)(2,1)S(1)} %collective-permute-done.recv, bf16[256,512]{1,0:T(8,128)(2,1)S(1)} %bitcast.37, ...), custom_call_target="tpu_custom_call" | custom-call | flops 1342177280 | bytes 8388608 | tf_op jit(solution)/shard_map/prompt_last/pallas_call | solution.py:244
  71.3 6.3 %collective-permute-start.4 = (bf16[128,2560]{1,0:T(8,128)(2,1)}, bf16[128,2560]{1,0:T(8,128)(2,1)S(1)}, u32[]{:S(2)}, u32[]{:S(2)}) collective-permute-start(bf16[128,2560]{1,0:T(8,128)(2,1)} %get-tuple-element.26), channel_id=1, source_target_pairs={{0,64},{64,0},{1,65},{65,1},{2,66},{66,2},{3,67},{67,3},{4,68},{68... | collective-permute-start | bytes 1966088 | tf_op jit(solution)/shard_map/ppermute | solution.py:257
  77.6 0.0 collective-permute-done.7
  77.7 0.0 collective-permute-done.6
  77.7 0.0 collective-permute-done.5
  77.7 0.9 add_convert_fusion
  78.5 5.9 %all-to-all-start.1 = ((bf16[16,16,512]{2,1,0:T(8,128)(2,1)}), bf16[16,16,512]{2,1,0:T(8,128)(2,1)S(1)}, u32[]{:S(2)}, u32[]{:S(2)}) async-start(bf16[16,16,512]{2,1,0:T(8,128)(2,1)} %bitcast.16), calls=%async_computation.1 | async-start | bytes 524288 | tf_op jit(solution)/shard_map/all_to_all | solution.py:260
  84.4 0.0 collective-permute-done.4
  84.5 1.2 %maximum_select_fusion = bf16[1,128,4096]{2,1,0:T(8,128)(2,1)} fusion(bf16[1,128,2048]{2,1,0:T(8,128)(2,1)S(1)} %slice_bitcast_fusion, bf16[1,128,2048]{2,1,0:T(8,128)(2,1)S(1)} %bitcast.41, pred[]{:T(512)S(6)} %eq.2), kind=kLoop, calls=%fused_computation | loop fusion | flops 4718592 | bytes 2097153 | tf_op jit(solution)/shard_map/jit(_where)/select_n | solution.py:268
  85.7 6.4 %all-to-all-done.1 = bf16[16,16,512]{2,1,0:T(8,128)(2,1)S(1)} async-done(((bf16[16,16,512]{2,1,0:T(8,128)(2,1)}), bf16[16,16,512]{2,1,0:T(8,128)(2,1)S(1)}, u32[]{:S(2)}, u32[]{:S(2)}) %all-to-all-start.1) | async-done | bytes 262176 | tf_op jit(solution)/shard_map/all_to_all | solution.py:260
  92.1 0.7 tile.5
  92.8 9.7 %all-to-all-start.2 = ((bf16[8,16,512]{2,1,0:T(8,128)(2,1)}), bf16[8,16,512]{2,1,0:T(8,128)(2,1)S(1)}, u32[]{:S(2)}, u32[]{:S(2)}) async-start(bf16[8,16,512]{2,1,0:T(8,128)(2,1)} %tile.5), calls=%async_computation.2 | async-start | bytes 262144 | tf_op jit(solution)/shard_map/all_to_all | solution.py:262
  102.5 0.7 maximum_select_fusion.2
  103.2 0.7 maximum_select_fusion.1
  103.9 6.7 %all-to-all-done.2 = bf16[8,16,512]{2,1,0:T(8,128)(2,1)S(1)} async-done(((bf16[8,16,512]{2,1,0:T(8,128)(2,1)}), bf16[8,16,512]{2,1,0:T(8,128)(2,1)S(1)}, u32[]{:S(2)}, u32[]{:S(2)}) %all-to-all-start.2) | async-done | bytes 131104 | tf_op jit(solution)/shard_map/all_to_all | solution.py:262
  110.6 0.2 reshape.205
  110.7 0.1 reduce_sum.22
  110.9 0.6 reshape.204
  111.6 0.6 reshape.203
  (18 shorter events, 0.2 us)
Async XLA Ops:
  0.6 19.6 %copy-start.6 = (bf16[16,512]{1,0:T(8,128)(2,1)S(1)}, bf16[16,512]{1,0:T(8,128)(2,1)}, u32[]{:S(2)}) copy-start(bf16[16,512]{1,0:T(8,128)(2,1)} %param.16) | copy-start | bytes 49156
  1.4 1.2 %copy-start = (bf16[1,128,4096]{2,1,0:T(8,128)(2,1)S(1)}, bf16[1,128,4096]{2,1,0:T(8,128)(2,1)}, u32[]{:S(2)}) copy-start(bf16[1,128,4096]{2,1,0:T(8,128)(2,1)} %param.9) | copy-start | bytes 3145732
  2.6 1.2 %copy-start.1 = (bf16[1,128,4096]{2,1,0:T(8,128)(2,1)S(1)}, bf16[1,128,4096]{2,1,0:T(8,128)(2,1)}, u32[]{:S(2)}) copy-start(bf16[1,128,4096]{2,1,0:T(8,128)(2,1)} %param.12) | copy-start | bytes 3145732
  3.8 1.2 %copy-start.2 = (bf16[1,128,4096]{2,1,0:T(8,128)(2,1)S(1)}, bf16[1,128,4096]{2,1,0:T(8,128)(2,1)}, u32[]{:S(2)}) copy-start(bf16[1,128,4096]{2,1,0:T(8,128)(2,1)} %param.13) | copy-start | bytes 3145732
  5.1 0.9 copy-start.3
  6.0 0.9 copy-start.4
  6.9 0.7 copy-start.5
  7.6 12.7 %copy-start.7 = (bf16[16,512]{1,0:T(8,128)(2,1)S(1)}, bf16[16,512]{1,0:T(8,128)(2,1)}, u32[]{:S(2)}) copy-start(bf16[16,512]{1,0:T(8,128)(2,1)} %param.15) | copy-start | bytes 49156
  11.5 32.9 %collective-permute-start = (bf16[2,2352,128]{2,1,0:T(8,128)(2,1)}, bf16[2,2352,128]{2,1,0:T(8,128)(2,1)S(1)}, u32[]{:S(2)}, u32[]{:S(2)}) collective-permute-start(bf16[2,2352,128]{2,1,0:T(8,128)(2,1)} %get-tuple-element.19), channel_id=1, source_target_pairs={{0,64},{64,0},{1,65},{65,1},{2,66},{66,2},{3,67},{67,3},{4,68},{68... | collective-permute-start | bytes 3612680 | tf_op jit(solution)/shard_map/ppermute | solution.py:203
  34.4 12.5 %collective-permute-start.3 = (bf16[256,512]{1,0:T(8,128)(2,1)S(1)}, bf16[256,512]{1,0:T(8,128)(2,1)S(1)}, u32[]{:S(2)}, u32[]{:S(2)}) collective-permute-start(bf16[256,512]{1,0:T(8,128)(2,1)S(1)} %bitcast.34), channel_id=1, source_target_pairs={{0,48},{16,0},{32,16},{48,32},{1,49},{17,1},{33,17},{49,33},{2,50}... | collective-permute-start | bytes 786440 | tf_op jit(solution)/shard_map/ppermute | solution.py:216
  38.8 11.7 %collective-permute-start.2 = (bf16[256,512]{1,0:T(8,128)(2,1)S(1)}, bf16[256,512]{1,0:T(8,128)(2,1)S(1)}, u32[]{:S(2)}, u32[]{:S(2)}) collective-permute-start(bf16[256,512]{1,0:T(8,128)(2,1)S(1)} %bitcast.35), channel_id=1, source_target_pairs={{0,16},{16,32},{32,48},{48,0},{1,17},{17,33},{33,49},{49,1},{2,18}... | collective-permute-start | bytes 786440 | tf_op jit(solution)/shard_map/ppermute | solution.py:216
  40.7 13.3 %collective-permute-start.1 = (bf16[256,512]{1,0:T(8,128)(2,1)S(1)}, bf16[256,512]{1,0:T(8,128)(2,1)S(1)}, u32[]{:S(2)}, u32[]{:S(2)}) collective-permute-start(bf16[256,512]{1,0:T(8,128)(2,1)S(1)} %bitcast.36), channel_id=1, source_target_pairs={{0,32},{16,48},{32,0},{48,16},{1,33},{17,49},{33,1},{49,17},{2,34}... | collective-permute-start | bytes 786440 | tf_op jit(solution)/shard_map/ppermute | solution.py:216
  57.5 20.1 %collective-permute-start.7 = (bf16[256,512]{1,0:T(8,128)(2,1)S(1)}, bf16[256,512]{1,0:T(8,128)(2,1)S(1)}, u32[]{:S(2)}, u32[]{:S(2)}) collective-permute-start(bf16[256,512]{1,0:T(8,128)(2,1)S(1)} %get-tuple-element.30), channel_id=1, source_target_pairs={{0,32},{16,48},{32,0},{48,16},{1,33},{17,49},{33,1},{49,17},{2,34}... | collective-permute-start | bytes 786440 | tf_op jit(solution)/shard_map/ppermute | solution.py:216
  60.7 17.0 %collective-permute-start.6 = (bf16[256,512]{1,0:T(8,128)(2,1)S(1)}, bf16[256,512]{1,0:T(8,128)(2,1)S(1)}, u32[]{:S(2)}, u32[]{:S(2)}) collective-permute-start(bf16[256,512]{1,0:T(8,128)(2,1)S(1)} %get-tuple-element.29), channel_id=1, source_target_pairs={{0,48},{16,0},{32,16},{48,32},{1,49},{17,1},{33,17},{49,33},{2,50}... | collective-permute-start | bytes 786440 | tf_op jit(solution)/shard_map/ppermute | solution.py:216
  65.3 12.4 %collective-permute-start.5 = (bf16[256,512]{1,0:T(8,128)(2,1)S(1)}, bf16[256,512]{1,0:T(8,128)(2,1)S(1)}, u32[]{:S(2)}, u32[]{:S(2)}) collective-permute-start(bf16[256,512]{1,0:T(8,128)(2,1)S(1)} %get-tuple-element.28), channel_id=1, source_target_pairs={{0,16},{16,32},{32,48},{48,0},{1,17},{17,33},{33,49},{49,1},{2,18}... | collective-permute-start | bytes 786440 | tf_op jit(solution)/shard_map/ppermute | solution.py:216
  71.3 13.2 %collective-permute-start.4 = (bf16[128,2560]{1,0:T(8,128)(2,1)}, bf16[128,2560]{1,0:T(8,128)(2,1)S(1)}, u32[]{:S(2)}, u32[]{:S(2)}) collective-permute-start(bf16[128,2560]{1,0:T(8,128)(2,1)} %get-tuple-element.26), channel_id=1, source_target_pairs={{0,64},{64,0},{1,65},{65,1},{2,66},{66,2},{3,67},{67,3},{4,68},{68... | collective-permute-start | bytes 1966088 | tf_op jit(solution)/shard_map/ppermute | solution.py:257
  78.5 13.6 %all-to-all-start.1 = ((bf16[16,16,512]{2,1,0:T(8,128)(2,1)}), bf16[16,16,512]{2,1,0:T(8,128)(2,1)S(1)}, u32[]{:S(2)}, u32[]{:S(2)}) async-start(bf16[16,16,512]{2,1,0:T(8,128)(2,1)} %bitcast.16), calls=%async_computation.1 | async-start | bytes 524288 | tf_op jit(solution)/shard_map/all_to_all | solution.py:260
  92.8 17.8 %all-to-all-start.2 = ((bf16[8,16,512]{2,1,0:T(8,128)(2,1)}), bf16[8,16,512]{2,1,0:T(8,128)(2,1)S(1)}, u32[]{:S(2)}, u32[]{:S(2)}) async-start(bf16[8,16,512]{2,1,0:T(8,128)(2,1)} %tile.5), calls=%async_computation.2 | async-start | bytes 262144 | tf_op jit(solution)/shard_map/all_to_all | solution.py:262

commit v2 on v1

v2 whole, which is shorter than its diff:
```python
import functools
import math

import jax
import jax.numpy as jnp
from jax import lax
from jax.experimental import pallas as pl
from jax.experimental.pallas import tpu as pltpu
from jax.sharding import Mesh
from jax.sharding import PartitionSpec as P

H = 32
KVH = 4
HD = 128
R = 128
G = H // KVH
QR = G * R
SCALE = HD**-0.5
LOG2E = math.log2(math.e)
AXES = ("yh", "core", "x", "yl", "zh", "zl")
f32 = jnp.float32
bf16 = jnp.bfloat16

OFF_DO = QR
OFF_K = 2 * QR
OFF_V = OFF_K + R
OFF_ST = OFF_V + R
PACK = OFF_ST + 6 * G

NT = (((1,), (1,)), ((), ()))
NN = (((1,), (0,)), ((), ()))
VMEM = pl.BlockSpec(memory_space=pltpu.VMEM)
SMEM = pl.BlockSpec(memory_space=pltpu.SMEM)
ANY = pl.BlockSpec(memory_space=pl.ANY)
FLIPS = (2, 1, 3)
CHUNK = 512


def dot(a, b, dims):
    return lax.dot_general(a, b, dims, preferred_element_type=f32)


def split3(value):
    hi = value.astype(bf16)
    rest = value - hi.astype(f32)
    mid = rest.astype(bf16)
    low = (rest - mid.astype(f32)).astype(bf16)
    return hi, mid, low


def prep_kernel(info, q, do, out, k, v, lse, order_by, send, mine, q_buf, do_buf, out_buf, k_buf, v_buf, sems, kv_sems):
    core = info[0]
    length = info[1]
    order = (2 * (1 - core), 2 * (1 - core) + 1, 2 * core, 2 * core + 1)
    wide = [
        [
            pltpu.make_async_copy(src.at[:, pl.ds(pl.multiple_of(g * QR, QR), QR)], buf.at[i], sems.at[j, i])
            for j, (src, buf) in enumerate(((q, q_buf), (do, do_buf), (out, out_buf)))
        ]
        for i, g in enumerate(order)
    ]
    narrow = [pltpu.make_async_copy(k, k_buf, kv_sems.at[0]), pltpu.make_async_copy(v, v_buf, kv_sems.at[1])]
    for copies in [narrow] + wide:
        for copy in copies:
            copy.start()
    for copy in narrow:
        copy.wait()
    ones = jnp.ones((8, HD), bf16)
    token = lax.broadcasted_iota(jnp.int32, (G, R), 1)
    for i, g in enumerate(order):
        ref = send if i < 2 else mine
        s = i % 2
        for copy in wide[i]:
            copy.wait()
        rows = []
        for h in range(G):
            cols = slice(h * HD, (h + 1) * HD)
            ref[s, h * R : (h + 1) * R, :] = q_buf[i, :, cols]
            dh = do_buf[i, :, cols]
            ref[s, OFF_DO + h * R : OFF_DO + (h + 1) * R, :] = dh
            prod = dh.astype(f32) * out_buf[i, :, cols].astype(f32)
            hi = prod.astype(bf16)
            low = (prod - hi.astype(f32)).astype(bf16)
            rows.append((dot(ones, hi, NT) + dot(ones, low, NT))[0:1, :])
        head = pl.ds(pl.multiple_of(g * HD, HD), HD)
        ref[s, OFF_K : OFF_K + R, :] = k_buf[:, head]
        ref[s, OFF_V : OFF_V + R, :] = v_buf[:, head]
        delta = jnp.concatenate(rows, 0)
        lse_g = lse[pl.ds(pl.multiple_of(g * G, G), G), :]
        lse2 = jnp.where(token < length, lse_g * LOG2E, 1e30)
        ref[s, OFF_ST:PACK, :] = jnp.concatenate(split3(lse2) + split3(delta), 0)


def prep(core, length, q, do, out, k, v, lse_t, order_by):
    shape = jax.ShapeDtypeStruct((2, PACK, HD), bf16)
    whole = pl.BlockSpec(memory_space=pl.ANY)
    wide = pltpu.VMEM((4, R, QR), bf16)
    narrow = pltpu.VMEM((R, KVH * HD), bf16)
    return pl.pallas_call(
        prep_kernel,
        out_shape=(shape, shape),
        in_specs=[pl.BlockSpec(memory_space=pltpu.SMEM)] + [whole] * 5 + [VMEM, whole],
        out_specs=(VMEM, VMEM),
        scratch_shapes=[wide, wide, wide, narrow, narrow, pltpu.SemaphoreType.DMA((3, 4)), pltpu.SemaphoreType.DMA((2,))],
        compiler_params=pltpu.CompilerParams(vmem_limit_bytes=61 * 2**20),
        cost_estimate=pl.CostEstimate(flops=10**7, bytes_accessed=8 * 2**20, transcendentals=0),
        name="prep",
    )(jnp.stack([core, length]), q, do, out, k, v, lse_t, order_by)


def stat_row(ref, g, kind, first, count):
    base = OFF_ST + kind * 3 * G
    block = [ref[g, base + term * G : base + (term + 1) * G, :].astype(f32) for term in range(3)]
    total = block[0] + block[1] + block[2]
    return jnp.concatenate([total[h : h + 1, :] for h in range(first, first + count)], 1)


def tile_grads(ref, g, chunk, keys, values, causal):
    cs = slice(chunk * CHUNK, (chunk + 1) * CHUNK)
    qc = ref[g, cs, :]
    dc = ref[g, OFF_DO + chunk * CHUNK : OFF_DO + (chunk + 1) * CHUNK, :]
    heads = CHUNK // R
    lse2 = stat_row(ref, g, 0, chunk * heads, heads)
    delta = stat_row(ref, g, 1, chunk * heads, heads)
    scores = dot(keys, qc, NT)
    prob_grad = dot(values, dc, NT)
    probs = jnp.exp2(scores * (SCALE * LOG2E) - lse2)
    if causal:
        shape = scores.shape
        token = lax.broadcasted_iota(jnp.int32, shape, 1) % R
        probs = jnp.where(lax.broadcasted_iota(jnp.int32, shape, 0) <= token, probs, 0.0)
    score_low = (probs * (prob_grad - delta)).astype(bf16)
    dv = dot(probs.astype(bf16), dc, NN)
    dk = dot(score_low, qc, NN)
    dq = lax.dot_general(keys, score_low, (((0,), (0,)), ((), ())), preferred_element_type=f32).T
    return dk, dv, dq, cs


def prompt_block(mine, recv, kv, emit_dq, out):
    rows = kv.shape[0]
    for g in range(2):
        keys = kv[:, g * HD : (g + 1) * HD]
        values = kv[:, (2 + g) * HD : (3 + g) * HD]
        dk = jnp.zeros((rows, HD), f32)
        dv = jnp.zeros((rows, HD), f32)
        for r, ref in enumerate((mine, recv)):
            for chunk in range(QR // CHUNK):
                dk_c, dv_c, dq_c, cs = tile_grads(ref, g, chunk, keys, values, False)
                dk += dk_c
                dv += dv_c
                emit_dq(r, g, cs, dq_c)
        out[:, g * HD : (g + 1) * HD] = (dk * SCALE).astype(out.dtype)
        out[:, (2 + g) * HD : (3 + g) * HD] = dv.astype(out.dtype)


def first_kernel(mine, recv, kv, dq, grads, out):
    for r, ref in enumerate((mine, recv)):
        for g in range(2):
            keys = ref[g, OFF_K : OFF_K + R, :]
            values = ref[g, OFF_V : OFF_V + R, :]
            dk = jnp.zeros((R, HD), f32)
            dv = jnp.zeros((R, HD), f32)
            for chunk in range(QR // CHUNK):
                dk_c, dv_c, dq_c, cs = tile_grads(ref, g, chunk, keys, values, True)
                dk += dk_c
                dv += dv_c
                dq[r, g, cs, :] = dq_c
            grads[r, :, g * HD : (g + 1) * HD] = (dk * SCALE).astype(bf16)
            grads[r, :, (2 + g) * HD : (3 + g) * HD] = dv.astype(bf16)

    def emit_dq(r, g, cs, value):
        dq[r, g, cs, :] += value

    prompt_block(mine, recv, kv, emit_dq, out)


def middle_kernel(mine, recv, kv_a, kv_b, dq_in, dq, out_a, out_b):
    def emit_a(r, g, cs, value):
        dq[r, g, cs, :] = dq_in[r, g, cs, :] + value

    def emit_b(r, g, cs, value):
        dq[r, g, cs, :] += value

    prompt_block(mine, recv, kv_a, emit_a, out_a)
    prompt_block(mine, recv, kv_b, emit_b, out_b)


def last_kernel(core, mine, recv, kv, dq_in, grads, order_by, back, out, full_dq, full_dk, full_dv, own, sems):
    def emit_dq(r, g, cs, value):
        total = ((dq_in[r, g, cs, :] + value) * SCALE).astype(bf16)
        target = own if r == 0 else back
        for j in range(CHUNK // R):
            h = g * G + cs.start // R + j
            target[:, h * HD : (h + 1) * HD] = total[j * R : (j + 1) * R, :]

    def place(full, width):
        return full.at[:, pl.ds(pl.multiple_of(core[0] * width, width), width)]

    half = 2 * HD
    copies = [
        pltpu.make_async_copy(grads.at[0, :, :half], place(full_dk, half), sems.at[0]),
        pltpu.make_async_copy(grads.at[0, :, half:], place(full_dv, half), sems.at[1]),
        pltpu.make_async_copy(own, place(full_dq, 2 * QR), sems.at[2]),
    ]
    copies[0].start()
    copies[1].start()
    prompt_block(mine, recv, kv, emit_dq, out)
    copies[2].start()
    back[:, 2 * QR :] = grads[1]
    for copy in copies:
        copy.wait()


def join_kernel(core, got, in_dq, in_dk, in_dv, full_dq, full_dk, full_dv, sems):
    half = 2 * HD
    other = 1 - core[0]
    copies = []
    for i, (full, start, width) in enumerate(
        ((full_dq, 0, 2 * QR), (full_dk, 2 * QR, half), (full_dv, 2 * QR + half, half))
    ):
        place = full.at[:, pl.ds(pl.multiple_of(other * width, width), width)]
        copies.append(pltpu.make_async_copy(got.at[:, start : start + width], place, sems.at[i]))
    for copy in copies:
        copy.start()
    for copy in copies:
        copy.wait()


def same_kernel(x, y, o, p):
    pass


def shard_kernel(core, k, v, o):
    rows = k.shape[0]
    cols = pl.ds(pl.multiple_of(core[0] * 2 * HD, 2 * HD), 2 * HD)
    shard = jnp.concatenate([k[:, cols], v[:, cols]], 1)
    for i in range(o.shape[0] // rows):
        o[i * rows : (i + 1) * rows, :] = shard


def sum_blocks_kernel(a, b, c, d, back_in, o, back):
    o[...] = (a[...] + b[...].astype(f32) + c[...].astype(f32) + d[...].astype(f32)).astype(bf16)


def sum_copies_kernel(x, o):
    rows = 16
    total = x[0:rows, :].astype(f32)
    for i in range(1, x.shape[0] // rows):
        total += x[i * rows : (i + 1) * rows, :].astype(f32)
    total = total.astype(bf16)
    for i in range(o.shape[0] // rows):
        o[i * rows : (i + 1) * rows, :] = total


def sum_samples_kernel(x, dk, dv):
    rows = 16
    half = 2 * HD
    for c in range(2):
        total = x[c * rows : (c + 1) * rows, :].astype(f32)
        for y in range(1, 4):
            at = (2 * y + c) * rows
            total += x[at : at + rows, :].astype(f32)
        dk[:, c * half : (c + 1) * half] = total[:, :half]
        dv[:, c * half : (c + 1) * half] = total[:, half:]


def simple(kernel, out_shape, name, *args, in_specs=None, out_specs=None, limit=16, **options):
    single = not isinstance(out_shape, tuple)
    return pl.pallas_call(
        kernel,
        out_shape=out_shape,
        in_specs=in_specs or [VMEM] * len(args),
        out_specs=out_specs or (VMEM if single else (VMEM,) * len(out_shape)),
        compiler_params=pltpu.CompilerParams(vmem_limit_bytes=limit * 2**20),
        name=name,
        **options,
    )(*args)


def cost(rows):
    return pl.CostEstimate(
        flops=5 * 2 * rows * 4 * QR * HD, bytes_accessed=8 * 2**20, transcendentals=rows * 4 * QR
    )


PARAMS = pltpu.CompilerParams(vmem_limit_bytes=24 * 2**20)


def body(resp_q, resp_k, resp_v, resp_do, resp_out, resp_lse, prompt_k, prompt_v, resp_lengths):
    core = lax.axis_index("core").astype(jnp.int32)
    rows = prompt_k.shape[0]
    outer = ("yl", "zh", "zl")
    inner = "x"

    shards = simple(
        shard_kernel,
        jax.ShapeDtypeStruct((16 * rows, 4 * HD), bf16),
        "shards",
        core[None],
        prompt_k,
        prompt_v,
        in_specs=[SMEM, VMEM, VMEM],
        limit=61,
    )
    kv0 = lax.all_to_all(shards, outer, 0, 0, tiled=True)
    send, mine = prep(
        core,
        resp_lengths[0],
        resp_q[0],
        resp_do[0],
        resp_out[0],
        resp_k[0],
        resp_v[0],
        resp_lse[0].T,
        shards,
    )
    kv0, send = simple(
        same_kernel,
        (jax.ShapeDtypeStruct(kv0.shape, bf16), jax.ShapeDtypeStruct(send.shape, bf16)),
        "gathered_and_prepared",
        kv0,
        send,
        in_specs=[ANY, ANY],
        out_specs=(ANY, ANY),
        input_output_aliases={0: 0, 1: 1},
        limit=63,
    )
    recv = lax.ppermute(send, "core", [(0, 1), (1, 0)])

    def along(value, flip):
        return lax.ppermute(value, inner, [(i, i ^ flip) for i in range(4)])

    block_rows = 16 * rows
    blocks = [along(kv0, flip) for flip in FLIPS]
    dq_shape = jax.ShapeDtypeStruct((2, 2, QR, HD), f32)
    part_shape = jax.ShapeDtypeStruct((block_rows, 4 * HD), bf16)
    options = dict(compiler_params=PARAMS)
    dq, grads, far = pl.pallas_call(
        first_kernel,
        out_shape=(dq_shape, jax.ShapeDtypeStruct((2, R, 4 * HD), bf16), part_shape),
        in_specs=[VMEM] * 3,
        out_specs=(VMEM,) * 3,
        cost_estimate=cost(R + block_rows),
        name="own_keys_and_far_block",
        **options,
    )(mine, recv, blocks[0])
    far = along(far, FLIPS[0])
    dq, near_a, near_b = pl.pallas_call(
        middle_kernel,
        out_shape=(dq_shape, part_shape, part_shape),
        in_specs=[VMEM] * 5,
        out_specs=(VMEM,) * 3,
        input_output_aliases={4: 0},
        cost_estimate=cost(2 * block_rows),
        name="near_blocks",
        **options,
    )(mine, recv, blocks[1], blocks[2], dq)
    near_a = along(near_a, FLIPS[1])
    near_b = along(near_b, FLIPS[2])
    narrow = jax.ShapeDtypeStruct((R, KVH * HD), bf16)
    back, part0, full_dq, full_dk, full_dv = pl.pallas_call(
        last_kernel,
        out_shape=(
            jax.ShapeDtypeStruct((R, 2 * QR + 4 * HD), bf16),
            jax.ShapeDtypeStruct((block_rows, 4 * HD), f32),
            jax.ShapeDtypeStruct((R, H * HD), bf16),
            narrow,
            narrow,
        ),
        in_specs=[SMEM] + [VMEM] * 5 + [ANY],
        out_specs=(VMEM, VMEM, ANY, ANY, ANY),
        scratch_shapes=[pltpu.VMEM((R, 2 * QR), bf16), pltpu.SemaphoreType.DMA((3,))],
        cost_estimate=cost(block_rows),
        name="own_block",
        **options,
    )(core[None], mine, recv, kv0, dq, grads, far)
    total, back = simple(
        sum_blocks_kernel,
        (part_shape, jax.ShapeDtypeStruct(back.shape, bf16)),
        "sum_blocks",
        part0,
        near_a,
        near_b,
        far,
        back,
        in_specs=[VMEM] * 4 + [ANY],
        out_specs=(VMEM, ANY),
        input_output_aliases={4: 1},
    )
    got = lax.ppermute(back, "core", [(0, 1), (1, 0)])
    total = lax.all_to_all(total, outer, 0, 0, tiled=True)
    total = simple(
        sum_copies_kernel, jax.ShapeDtypeStruct((8 * rows, 4 * HD), bf16), "sum_copies", total
    )
    total = lax.all_to_all(total, ("yh", "core"), 0, 0, tiled=True)
    final = jax.ShapeDtypeStruct((rows, KVH * HD), f32)
    prompt_dk, prompt_dv = simple(sum_samples_kernel, (final, final), "sum_samples", total)
    resp_dq, resp_dk, resp_dv = simple(
        join_kernel,
        (jax.ShapeDtypeStruct((R, H * HD), bf16), narrow, narrow),
        "join",
        core[None],
        got,
        full_dq,
        full_dk,
        full_dv,
        in_specs=[SMEM] + [ANY] * 4,
        out_specs=(ANY,) * 3,
        scratch_shapes=[pltpu.SemaphoreType.DMA((3,))],
        input_output_aliases={2: 0, 3: 1, 4: 2},
    )
    return resp_dq[None], resp_dk[None], resp_dv[None], prompt_dk, prompt_dv


def solution(mesh):
    fine = Mesh(mesh.devices.reshape(4, 2, 4, 2, 4, 2), AXES)
    both = P(AXES, None, None)
    prefix = P(("x", "yl", "zh", "zl"), None)
    return jax.shard_map(
        body,
        mesh=fine,
        in_specs=(both,) * 6 + (prefix, prefix, P(AXES)),
        out_specs=(both, both, both, prefix, prefix),
        check_vma=False,
    )
```

time: 113 us -> 102 us (0.903)
  blocking collectives: 14.1 us -> 0 us
  local copies, waits for them, and re-layouts: 8.48 us -> 1.99 us
  Pallas kernels: 20.9 us -> 25.5 us
  starting transfers between devices: 50.5 us -> 54.7 us
  waiting for transfers between devices: 13 us -> 17.2 us
  other arithmetic: 3.67 us -> 0.59 us
    all_to_all x1 -> x0, blocking collectives: 14.1 us -> none  [body(): kv0 = lax.all_to_all(jnp.tile(shard, (16, 1)), inner, 0, 0, tiled=True)]
    all_to_all x2 -> x3, starting transfers between devices: 15.6 us -> 26 us  [the longest x1 12 us: body(): kv0 = lax.all_to_all(shards, outer, 0, 0, tiled=True)]
    ppermute x6, waiting for transfers between devices: 0.02 us -> 5.39 us  [along(): return lax.ppermute(value, inner, [(i, i ^ flip) for i in range(4)])]
    pallas_call x6 -> x10, Pallas kernels: 20.9 us -> 25.5 us  [the longest x1 6.35 us: body(): pl.pallas_call(middle_kernel, out_shape=(dq_shape, part_shape, part_shape...]
    unnamed x18 -> x8, local copies, waits for them, and re-layouts: 6.21 us -> 1.99 us
    ppermute x1, starting transfers between devices: 8.77 us -> 5.22 us  [body(): recv = lax.ppermute(send, 'core', [(0, 1), (1, 0)])]
    select_n x3 -> x0, other arithmetic: 2.58 us -> none  [join(): jnp.where(core == 0, jnp.concatenate([first, second], -1), jnp.concatenat...]
    ppermute x1, starting transfers between devices: 6.33 us -> 4.53 us  [body(): got = lax.ppermute(back, 'core', [(0, 1), (1, 0)])]
  transfers between devices with their start and end apart: 10 -> 11, of which waited for: 2 -> 5; matrix products, arithmetic and copies ran while one was open for 3% -> 1% of each run, Pallas kernels for 12% -> 22%
where the time goes in v2:
time: 102 us; the launch traced here: 101 us
  starting transfers between devices  54.7 us (54%)
  Pallas kernels  25.5 us (25%)
  waiting for transfers between devices  17.2 us (17%)
  local copies, waits for them, and re-layouts  1.99 us (2%)
  between operations  1.47 us (1%)
    ppermute x6, starting transfers between devices, along(): return lax.ppermute(value, inner, [(i, i ^ flip) for i in range(4)])  18.9 us
    all_to_all x1, starting transfers between devices, body(): kv0 = lax.all_to_all(shards, outer, 0, 0, tiled=True)  12 us
    all_to_all x1, starting transfers between devices, body(): total = lax.all_to_all(total, ('yh', 'core'), 0, 0, tiled=True)  10 us
    all_to_all x1, waiting for transfers between devices, body(): total = lax.all_to_all(total, ('yh', 'core'), 0, 0, tiled=True)  7.19 us
    pallas_call x1, Pallas kernels, body(): pl.pallas_call(middle_kernel, out_shape=(dq_shape, part_shape, part_shape...  6.35 us
    pallas_call x1, Pallas kernels, prep(): pl.pallas_call(prep_kernel, out_shape=(shape, shape), in_specs=[pl.BlockS...  5.55 us
    pallas_call x1, Pallas kernels, body(): pl.pallas_call(first_kernel, out_shape=(dq_shape, jax.ShapeDtypeStruct((2...  5.44 us
    ppermute x6, waiting for transfers between devices, along(): return lax.ppermute(value, inner, [(i, i ^ flip) for i in range(4)])  5.39 us
  transfers between devices with their start and end apart: 11, of which 5 were waited for; matrix products, arithmetic and copies ran while one was open for 1% of the time, Pallas kernels for 22%

profile of v2, /device:TPU:1, one launch (start us, length us, event | category | flops | bytes accessed | tf_op | source)
XLA Modules:
  0.0 101.5 jit_solution(5883802708813856857)
XLA Ops:
  0.6 1.5 %shards.1.order_by = bf16[256,512]{1,0:T(8,128)(2,1)} custom-call(s32[1]{0:T(128)} %bitcast.core, bf16[16,512]{1,0:T(8,128)(2,1)} %k.1, bf16[16,512]{1,0:T(8,128)(2,1)} %v.1), custom_call_target="tpu_custom_call" | custom-call | tf_op jit(solution)/shard_map/shards/pallas_call | solution.py:269
  2.1 12.0 %all-to-all-start = ((bf16[16,16,512]{2,1,0:T(8,128)(2,1)}), bf16[16,16,512]{2,1,0:T(8,128)(2,1)S(1)}, u32[]{:S(2)}, u32[]{:S(2)}) async-start(bf16[16,16,512]{2,1,0:T(8,128)(2,1)} %bitcast.21), calls=%async_computation | async-start | bytes 524288 | tf_op jit(solution)/shard_map/all_to_all | solution.py:305
  14.7 0.6 pad_add_fusion.info
  15.3 5.5 %prep.1 = (bf16[2,2352,128]{2,1,0:T(8,128)(2,1)}, bf16[2,2352,128]{2,1,0:T(8,128)(2,1)}) custom-call(s32[2]{0:T(128)} %pad_add_fusion.info, bf16[128,4096]{1,0:T(8,128)(2,1)} %bitcast.23, bf16[128,4096]{1,0:T(8,128)(2,1)} %bitcast.24, bf16[128,4096]{1,0:T(8,128)(2,1)} %bitcast.25, bf16[128,512]{1,0:T(8,128)(2,1)} %bitcast.26, bf16[128,512]{1,0:T(8,128)(2,1)} %bitcast.27, ...), custom_call_target="tpu_custom_call" | custom-call | flops 10000000 | bytes 8388608 | tf_op jit(solution)/shard_map/prep/pallas_call | solution.py:99
  20.9 1.5 %all-to-all-done = bf16[16,16,512]{2,1,0:T(8,128)(2,1)S(1)} async-done(((bf16[16,16,512]{2,1,0:T(8,128)(2,1)}), bf16[16,16,512]{2,1,0:T(8,128)(2,1)S(1)}, u32[]{:S(2)}, u32[]{:S(2)}) %all-to-all-start) | async-done | bytes 262176 | tf_op jit(solution)/shard_map/all_to_all | solution.py:305
  22.4 0.0 copy-start
  22.4 0.7 copy-done
  23.1 5.2 %collective-permute-start = (bf16[2,2352,128]{2,1,0:T(8,128)(2,1)}, bf16[2,2352,128]{2,1,0:T(8,128)(2,1)S(1)}, u32[]{:S(2)}, u32[]{:S(2)}) collective-permute-start(bf16[2,2352,128]{2,1,0:T(8,128)(2,1)} %get-tuple-element.29), channel_id=1, source_target_pairs={{0,64},{64,0},{1,65},{65,1},{2,66},{66,2},{3,67},{67,3},{4,68},{68... | collective-permute-start | bytes 3612680 | tf_op jit(solution)/shard_map/ppermute | solution.py:328
  28.3 4.7 %collective-permute-start.3 = (bf16[256,512]{1,0:T(8,128)(2,1)}, bf16[256,512]{1,0:T(8,128)(2,1)S(1)}, u32[]{:S(2)}, u32[]{:S(2)}) collective-permute-start(bf16[256,512]{1,0:T(8,128)(2,1)} %get-tuple-element.30.kv), channel_id=1, source_target_pairs={{0,32},{16,48},{32,0},{48,16},{1,33},{17,49},{33,1},{49,17},{2,34}... | collective-permute-start | bytes 786440 | tf_op jit(solution)/shard_map/ppermute | solution.py:331
  33.0 2.8 %collective-permute-start.2 = (bf16[256,512]{1,0:T(8,128)(2,1)}, bf16[256,512]{1,0:T(8,128)(2,1)S(1)}, u32[]{:S(2)}, u32[]{:S(2)}) collective-permute-start(bf16[256,512]{1,0:T(8,128)(2,1)} %get-tuple-element.30.kv), channel_id=1, source_target_pairs={{0,48},{16,32},{32,16},{48,0},{1,49},{17,33},{33,17},{49,1},{2,50}... | collective-permute-start | bytes 786440 | tf_op jit(solution)/shard_map/ppermute | solution.py:331
  35.8 1.9 %collective-permute-start.1 = (bf16[256,512]{1,0:T(8,128)(2,1)}, bf16[256,512]{1,0:T(8,128)(2,1)S(1)}, u32[]{:S(2)}, u32[]{:S(2)}) collective-permute-start(bf16[256,512]{1,0:T(8,128)(2,1)} %get-tuple-element.30.kv), channel_id=1, source_target_pairs={{0,16},{16,0},{32,48},{48,32},{1,17},{17,1},{33,49},{49,33},{2,18}... | collective-permute-start | bytes 786440 | tf_op jit(solution)/shard_map/ppermute | solution.py:331
  37.7 2.2 %collective-permute-done.3.kv = bf16[256,512]{1,0:T(8,128)(2,1)S(1)} collective-permute-done((bf16[256,512]{1,0:T(8,128)(2,1)}, bf16[256,512]{1,0:T(8,128)(2,1)S(1)}, u32[]{:S(2)}, u32[]{:S(2)}) %collective-permute-start.3) | collective-permute-done | bytes 262176 | tf_op jit(solution)/shard_map/ppermute | solution.py:331
  39.9 0.0 collective-permute-done.recv
  39.9 0.0 copy-start.2
  39.9 1.3 %copy-done.2 = bf16[2,2352,128]{2,1,0:T(8,128)(2,1)S(1)} copy-done((bf16[2,2352,128]{2,1,0:T(8,128)(2,1)S(1)}, bf16[2,2352,128]{2,1,0:T(8,128)(2,1)}, u32[]{:S(2)}) %copy-start.2) | copy-done | bytes 1204248
  41.1 5.4 %own_keys_and_far_block.1 = (f32[2,2,1024,128]{3,2,1,0:T(8,128)S(1)}, bf16[2,128,512]{2,1,0:T(8,128)(2,1)S(1)}, bf16[256,512]{1,0:T(8,128)(2,1)S(1)}) custom-call(bf16[2,2352,128]{2,1,0:T(8,128)(2,1)S(1)} %copy-done.2, bf16[2,2352,128]{2,1,0:T(8,128)(2,1)S(1)} %collective-permute-done.recv, bf16[256,512]{1,0:T(8,128)(2,1)S(1)} %collective-permute-done.3.kv), custom_call_target="tpu_custom_call" | custom-call | flops 2013265920 | bytes 8388608 | tf_op jit(solution)/shard_map/own_keys_and_far_block/pallas_call | solution.py:338
  46.6 4.9 %collective-permute-start.4 = (bf16[256,512]{1,0:T(8,128)(2,1)S(1)}, bf16[256,512]{1,0:T(8,128)(2,1)S(1)}, u32[]{:S(2)}, u32[]{:S(2)}) collective-permute-start(bf16[256,512]{1,0:T(8,128)(2,1)S(1)} %get-tuple-element.34), channel_id=1, source_target_pairs={{0,32},{16,48},{32,0},{48,16},{1,33},{17,49},{33,1},{49,17},{2,34}... | collective-permute-start | bytes 786440 | tf_op jit(solution)/shard_map/ppermute | solution.py:331
  51.5 0.0 collective-permute-done.2.kv_b
  51.5 0.0 collective-permute-done.1.kv_a
  51.5 0.0 copy-start.1
  51.5 0.0 copy-start.3
  51.5 6.4 %near_blocks.1 = (f32[2,2,1024,128]{3,2,1,0:T(8,128)S(1)}, bf16[256,512]{1,0:T(8,128)(2,1)S(1)}, bf16[256,512]{1,0:T(8,128)(2,1)S(1)}) custom-call(bf16[2,2352,128]{2,1,0:T(8,128)(2,1)S(1)} %copy-done.2, bf16[2,2352,128]{2,1,0:T(8,128)(2,1)S(1)} %collective-permute-done.recv, ...), custom_call_target="tpu_custom_call", output_to_operand_aliasing={{0}: (4, {})} | custom-call | flops 2684354560 | bytes 8388608 | tf_op jit(solution)/shard_map/near_blocks/pallas_call | solution.py:348
  57.9 2.2 %collective-permute-start.5 = (bf16[256,512]{1,0:T(8,128)(2,1)S(1)}, bf16[256,512]{1,0:T(8,128)(2,1)S(1)}, u32[]{:S(2)}, u32[]{:S(2)}) collective-permute-start(bf16[256,512]{1,0:T(8,128)(2,1)S(1)} %get-tuple-element.36), channel_id=1, source_target_pairs={{0,16},{16,0},{32,48},{48,32},{1,17},{17,1},{33,49},{49,33},{2,18}... | collective-permute-start | bytes 786440 | tf_op jit(solution)/shard_map/ppermute | solution.py:331
  60.1 2.5 %collective-permute-start.6 = (bf16[256,512]{1,0:T(8,128)(2,1)S(1)}, bf16[256,512]{1,0:T(8,128)(2,1)S(1)}, u32[]{:S(2)}, u32[]{:S(2)}) collective-permute-start(bf16[256,512]{1,0:T(8,128)(2,1)S(1)} %get-tuple-element.37), channel_id=1, source_target_pairs={{0,48},{16,32},{32,16},{48,0},{1,49},{17,33},{33,17},{49,1},{2,50}... | collective-permute-start | bytes 786440 | tf_op jit(solution)/shard_map/ppermute | solution.py:331
  62.6 0.0 collective-permute-done.4.order_by.d
  62.6 0.0 copy-done.1
  62.6 0.0 copy-done.3
  62.6 3.7 %own_block.1 = (bf16[128,2560]{1,0:T(8,128)(2,1)S(1)}, f32[256,512]{1,0:T(8,128)S(1)}, bf16[128,4096]{1,0:T(8,128)(2,1)}, bf16[128,512]{1,0:T(8,128)(2,1)}, bf16[128,512]{1,0:T(8,128)(2,1)}) custom-call(s32[1]{0:T(128)} %bitcast.core, bf16[2,2352,128]{2,1,0:T(8,128)(2,1)S(1)} %copy-done.3, bf16[2,2352,128]{2,1,0:T(8,128)(2,1)S(1)} %collective-permute-done.recv, ...), custom_call_target="tpu_custom_call" | custom-call | flops 1342177280 | bytes 8388608 | tf_op jit(solution)/shard_map/own_block/pallas_call | solution.py:361
  66.4 0.0 collective-permute-done.5.b
  66.4 3.2 %collective-permute-done.6.c = bf16[256,512]{1,0:T(8,128)(2,1)S(1)} collective-permute-done((bf16[256,512]{1,0:T(8,128)(2,1)S(1)}, bf16[256,512]{1,0:T(8,128)(2,1)S(1)}, u32[]{:S(2)}, u32[]{:S(2)}) %collective-permute-start.6) | collective-permute-done | bytes 262176 | tf_op jit(solution)/shard_map/ppermute | solution.py:331
  69.6 0.8 sum_blocks.1
  70.4 4.0 %all-to-all-start.1 = ((bf16[16,16,512]{2,1,0:T(8,128)(2,1)}), bf16[16,16,512]{2,1,0:T(8,128)(2,1)S(1)}, u32[]{:S(2)}, u32[]{:S(2)}) async-start(bf16[16,16,512]{2,1,0:T(8,128)(2,1)} %bitcast.13), calls=%async_computation.1 | async-start | bytes 524288 | tf_op jit(solution)/shard_map/all_to_all | solution.py:391
  74.4 4.5 %collective-permute-start.7 = (bf16[128,2560]{1,0:T(8,128)(2,1)S(1)}, bf16[128,2560]{1,0:T(8,128)(2,1)S(1)}, u32[]{:S(2)}, u32[]{:S(2)}) collective-permute-start(bf16[128,2560]{1,0:T(8,128)(2,1)S(1)} %get-tuple-element.39), channel_id=1, source_target_pairs={{0,64},{64,0},{1,65},{65,1},{2,66},{66,2},{3,67},{67,3},{4,68},{68... | collective-permute-start | bytes 1966088 | tf_op jit(solution)/shard_map/ppermute | solution.py:390
  78.9 3.1 %all-to-all-done.1 = bf16[16,16,512]{2,1,0:T(8,128)(2,1)S(1)} async-done(((bf16[16,16,512]{2,1,0:T(8,128)(2,1)}), bf16[16,16,512]{2,1,0:T(8,128)(2,1)S(1)}, u32[]{:S(2)}, u32[]{:S(2)}) %all-to-all-start.1) | async-done | bytes 262176 | tf_op jit(solution)/shard_map/all_to_all | solution.py:391
  82.1 0.7 sum_copies.1
  82.7 10.0 %all-to-all-start.2 = ((bf16[8,16,512]{2,1,0:T(8,128)(2,1)}), bf16[8,16,512]{2,1,0:T(8,128)(2,1)S(1)}, u32[]{:S(2)}, u32[]{:S(2)}) async-start(bf16[8,16,512]{2,1,0:T(8,128)(2,1)} %bitcast.15), calls=%async_computation.2 | async-start | bytes 262144 | tf_op jit(solution)/shard_map/all_to_all | solution.py:395
  92.8 0.0 collective-permute-done.7.got
  92.8 0.8 join.1
  93.6 7.2 %all-to-all-done.2 = bf16[8,16,512]{2,1,0:T(8,128)(2,1)S(1)} async-done(((bf16[8,16,512]{2,1,0:T(8,128)(2,1)}), bf16[8,16,512]{2,1,0:T(8,128)(2,1)S(1)}, u32[]{:S(2)}, u32[]{:S(2)}) %all-to-all-start.2) | async-done | bytes 131104 | tf_op jit(solution)/shard_map/all_to_all | solution.py:395
  100.8 0.6 sum_samples.1
  (1 shorter events, 0.0 us)
Async XLA Ops:
  2.1 20.3 %all-to-all-start = ((bf16[16,16,512]{2,1,0:T(8,128)(2,1)}), bf16[16,16,512]{2,1,0:T(8,128)(2,1)S(1)}, u32[]{:S(2)}, u32[]{:S(2)}) async-start(bf16[16,16,512]{2,1,0:T(8,128)(2,1)} %bitcast.21), calls=%async_computation | async-start | bytes 524288 | tf_op jit(solution)/shard_map/all_to_all | solution.py:305
  22.4 0.7 copy-start
  23.1 16.8 %collective-permute-start = (bf16[2,2352,128]{2,1,0:T(8,128)(2,1)}, bf16[2,2352,128]{2,1,0:T(8,128)(2,1)S(1)}, u32[]{:S(2)}, u32[]{:S(2)}) collective-permute-start(bf16[2,2352,128]{2,1,0:T(8,128)(2,1)} %get-tuple-element.29), channel_id=1, source_target_pairs={{0,64},{64,0},{1,65},{65,1},{2,66},{66,2},{3,67},{67,3},{4,68},{68... | collective-permute-start | bytes 3612680 | tf_op jit(solution)/shard_map/ppermute | solution.py:328
  28.3 11.5 %collective-permute-start.3 = (bf16[256,512]{1,0:T(8,128)(2,1)}, bf16[256,512]{1,0:T(8,128)(2,1)S(1)}, u32[]{:S(2)}, u32[]{:S(2)}) collective-permute-start(bf16[256,512]{1,0:T(8,128)(2,1)} %get-tuple-element.30.kv), channel_id=1, source_target_pairs={{0,32},{16,48},{32,0},{48,16},{1,33},{17,49},{33,1},{49,17},{2,34}... | collective-permute-start | bytes 786440 | tf_op jit(solution)/shard_map/ppermute | solution.py:331
  33.0 18.5 %collective-permute-start.2 = (bf16[256,512]{1,0:T(8,128)(2,1)}, bf16[256,512]{1,0:T(8,128)(2,1)S(1)}, u32[]{:S(2)}, u32[]{:S(2)}) collective-permute-start(bf16[256,512]{1,0:T(8,128)(2,1)} %get-tuple-element.30.kv), channel_id=1, source_target_pairs={{0,48},{16,32},{32,16},{48,0},{1,49},{17,33},{33,17},{49,1},{2,50}... | collective-permute-start | bytes 786440 | tf_op jit(solution)/shard_map/ppermute | solution.py:331
  35.8 15.7 %collective-permute-start.1 = (bf16[256,512]{1,0:T(8,128)(2,1)}, bf16[256,512]{1,0:T(8,128)(2,1)S(1)}, u32[]{:S(2)}, u32[]{:S(2)}) collective-permute-start(bf16[256,512]{1,0:T(8,128)(2,1)} %get-tuple-element.30.kv), channel_id=1, source_target_pairs={{0,16},{16,0},{32,48},{48,32},{1,17},{17,1},{33,49},{49,33},{2,18}... | collective-permute-start | bytes 786440 | tf_op jit(solution)/shard_map/ppermute | solution.py:331
  39.9 1.3 %copy-start.2 = (bf16[2,2352,128]{2,1,0:T(8,128)(2,1)S(1)}, bf16[2,2352,128]{2,1,0:T(8,128)(2,1)}, u32[]{:S(2)}) copy-start(bf16[2,2352,128]{2,1,0:T(8,128)(2,1)} %get-tuple-element.27.mine) | copy-start | bytes 3612676
  46.6 16.0 %collective-permute-start.4 = (bf16[256,512]{1,0:T(8,128)(2,1)S(1)}, bf16[256,512]{1,0:T(8,128)(2,1)S(1)}, u32[]{:S(2)}, u32[]{:S(2)}) collective-permute-start(bf16[256,512]{1,0:T(8,128)(2,1)S(1)} %get-tuple-element.34), channel_id=1, source_target_pairs={{0,32},{16,48},{32,0},{48,16},{1,33},{17,49},{33,1},{49,17},{2,34}... | collective-permute-start | bytes 786440 | tf_op jit(solution)/shard_map/ppermute | solution.py:331
  51.5 11.1 %copy-start.1 = (bf16[256,512]{1,0:T(8,128)(2,1)S(1)}, bf16[256,512]{1,0:T(8,128)(2,1)}, u32[]{:S(2)}) copy-start(bf16[256,512]{1,0:T(8,128)(2,1)} %get-tuple-element.30.kv) | copy-start | bytes 786436
  51.5 11.1 %copy-start.3 = (bf16[2,2352,128]{2,1,0:T(8,128)(2,1)S(1)}, bf16[2,2352,128]{2,1,0:T(8,128)(2,1)}, u32[]{:S(2)}) copy-start(bf16[2,2352,128]{2,1,0:T(8,128)(2,1)} %get-tuple-element.27.mine) | copy-start | bytes 3612676
  57.9 8.5 %collective-permute-start.5 = (bf16[256,512]{1,0:T(8,128)(2,1)S(1)}, bf16[256,512]{1,0:T(8,128)(2,1)S(1)}, u32[]{:S(2)}, u32[]{:S(2)}) collective-permute-start(bf16[256,512]{1,0:T(8,128)(2,1)S(1)} %get-tuple-element.36), channel_id=1, source_target_pairs={{0,16},{16,0},{32,48},{48,32},{1,17},{17,1},{33,49},{49,33},{2,18}... | collective-permute-start | bytes 786440 | tf_op jit(solution)/shard_map/ppermute | solution.py:331
  60.1 9.5 %collective-permute-start.6 = (bf16[256,512]{1,0:T(8,128)(2,1)S(1)}, bf16[256,512]{1,0:T(8,128)(2,1)S(1)}, u32[]{:S(2)}, u32[]{:S(2)}) collective-permute-start(bf16[256,512]{1,0:T(8,128)(2,1)S(1)} %get-tuple-element.37), channel_id=1, source_target_pairs={{0,48},{16,32},{32,16},{48,0},{1,49},{17,33},{33,17},{49,1},{2,50}... | collective-permute-start | bytes 786440 | tf_op jit(solution)/shard_map/ppermute | solution.py:331
  70.4 11.7 %all-to-all-start.1 = ((bf16[16,16,512]{2,1,0:T(8,128)(2,1)}), bf16[16,16,512]{2,1,0:T(8,128)(2,1)S(1)}, u32[]{:S(2)}, u32[]{:S(2)}) async-start(bf16[16,16,512]{2,1,0:T(8,128)(2,1)} %bitcast.13), calls=%async_computation.1 | async-start | bytes 524288 | tf_op jit(solution)/shard_map/all_to_all | solution.py:391
  74.4 18.4 %collective-permute-start.7 = (bf16[128,2560]{1,0:T(8,128)(2,1)S(1)}, bf16[128,2560]{1,0:T(8,128)(2,1)S(1)}, u32[]{:S(2)}, u32[]{:S(2)}) collective-permute-start(bf16[128,2560]{1,0:T(8,128)(2,1)S(1)} %get-tuple-element.39), channel_id=1, source_target_pairs={{0,64},{64,0},{1,65},{65,1},{2,66},{66,2},{3,67},{67,3},{4,68},{68... | collective-permute-start | bytes 1966088 | tf_op jit(solution)/shard_map/ppermute | solution.py:390
  82.7 18.1 %all-to-all-start.2 = ((bf16[8,16,512]{2,1,0:T(8,128)(2,1)}), bf16[8,16,512]{2,1,0:T(8,128)(2,1)S(1)}, u32[]{:S(2)}, u32[]{:S(2)}) async-start(bf16[8,16,512]{2,1,0:T(8,128)(2,1)} %bitcast.15), calls=%async_computation.2 | async-start | bytes 262144 | tf_op jit(solution)/shard_map/all_to_all | solution.py:395

commit v3 on v2

--- a/solution.py
+++ b/solution.py
@@ -32,7 +32,6 @@
 VMEM = pl.BlockSpec(memory_space=pltpu.VMEM)
 SMEM = pl.BlockSpec(memory_space=pltpu.SMEM)
 ANY = pl.BlockSpec(memory_space=pl.ANY)
-FLIPS = (2, 1, 3)
 CHUNK = 512
 
 
@@ -153,8 +152,37 @@
         out[:, (2 + g) * HD : (3 + g) * HD] = dv.astype(out.dtype)
 
 
-def first_kernel(mine, recv, kv, dq, grads, out):
-    for r, ref in enumerate((mine, recv)):
+def first_kernel(mine, recv, kv, dq, out):
+    def emit_dq(r, g, cs, value):
+        dq[r, g, cs, :] = value
+
+    prompt_block(mine, recv, kv, emit_dq, out)
+
+
+def middle_kernel(count, mine, recv, *refs):
+    kvs, dq_in, dq, outs = refs[:count], refs[count], refs[count + 1], refs[count + 2 :]
+    for i, (kv, out) in enumerate(zip(kvs, outs)):
+
+        def emit_dq(r, g, cs, value):
+            source = dq if i else dq_in
+            dq[r, g, cs, :] = source[r, g, cs, :] + value
+
+        prompt_block(mine, recv, kv, emit_dq, out)
+
+
+def last_kernel(core, mine, recv, dq_in, order_by, back, full_dq, full_dk, full_dv, own, grads, sems):
+    half = 2 * HD
+
+    def place(full, width):
+        return full.at[:, pl.ds(pl.multiple_of(core[0] * width, width), width)]
+
+    copies = [
+        pltpu.make_async_copy(own, place(full_dq, 2 * QR), sems.at[0]),
+        pltpu.make_async_copy(grads.at[:, :half], place(full_dk, half), sems.at[1]),
+        pltpu.make_async_copy(grads.at[:, half:], place(full_dv, half), sems.at[2]),
+    ]
+    for r, (ref, target) in enumerate(((mine, own), (recv, back))):
+        dest, base = (grads, 0) if r == 0 else (back, 2 * QR)
         for g in range(2):
             keys = ref[g, OFF_K : OFF_K + R, :]
             values = ref[g, OFF_V : OFF_V + R, :]
@@ -164,49 +192,15 @@
                 dk_c, dv_c, dq_c, cs = tile_grads(ref, g, chunk, keys, values, True)
                 dk += dk_c
                 dv += dv_c
-                dq[r, g, cs, :] = dq_c
-            grads[r, :, g * HD : (g + 1) * HD] = (dk * SCALE).astype(bf16)
-            grads[r, :, (2 + g) * HD : (3 + g) * HD] = dv.astype(bf16)
-
-    def emit_dq(r, g, cs, value):
-        dq[r, g, cs, :] += value
-
-    prompt_block(mine, recv, kv, emit_dq, out)
-
-
-def middle_kernel(mine, recv, kv_a, kv_b, dq_in, dq, out_a, out_b):
-    def emit_a(r, g, cs, value):
-        dq[r, g, cs, :] = dq_in[r, g, cs, :] + value
-
-    def emit_b(r, g, cs, value):
-        dq[r, g, cs, :] += value
-
-    prompt_block(mine, recv, kv_a, emit_a, out_a)
-    prompt_block(mine, recv, kv_b, emit_b, out_b)
-
-
-def last_kernel(core, mine, recv, kv, dq_in, grads, order_by, back, out, full_dq, full_dk, full_dv, own, sems):
-    def emit_dq(r, g, cs, value):
-        total = ((dq_in[r, g, cs, :] + value) * SCALE).astype(bf16)
-        target = own if r == 0 else back
-        for j in range(CHUNK // R):
-            h = g * G + cs.start // R + j
-            target[:, h * HD : (h + 1) * HD] = total[j * R : (j + 1) * R, :]
-
-    def place(full, width):
-        return full.at[:, pl.ds(pl.multiple_of(core[0] * width, width), width)]
-
-    half = 2 * HD
-    copies = [
-        pltpu.make_async_copy(grads.at[0, :, :half], place(full_dk, half), sems.at[0]),
-        pltpu.make_async_copy(grads.at[0, :, half:], place(full_dv, half), sems.at[1]),
-        pltpu.make_async_copy(own, place(full_dq, 2 * QR), sems.at[2]),
-    ]
-    copies[0].start()
-    copies[1].start()
-    prompt_block(mine, recv, kv, emit_dq, out)
-    copies[2].start()
-    back[:, 2 * QR :] = grads[1]
+                total = ((dq_in[r, g, cs, :] + dq_c) * SCALE).astype(bf16)
+                for j in range(CHUNK // R):
+                    h = g * G + chunk * (CHUNK // R) + j
+                    target[:, h * HD : (h + 1) * HD] = total[j * R : (j + 1) * R, :]
+            dest[:, base + g * HD : base + (g + 1) * HD] = (dk * SCALE).astype(bf16)
+            dest[:, base + (2 + g) * HD : base + (3 + g) * HD] = dv.astype(bf16)
+        if r == 0:
+            for copy in copies:
+                copy.start()
     for copy in copies:
         copy.wait()
 
@@ -271,7 +265,7 @@
         out_shape=out_shape,
         in_specs=in_specs or [VMEM] * len(args),
         out_specs=out_specs or (VMEM if single else (VMEM,) * len(out_shape)),
-        compiler_params=pltpu.CompilerParams(vmem_limit_bytes=limit * 2**20),
+        compiler_params=pltpu.CompilerParams(vmem_limit_bytes=int(limit * 2**20)),
         name=name,
         **options,
     )(*args)
@@ -323,7 +317,7 @@
         in_specs=[ANY, ANY],
         out_specs=(ANY, ANY),
         input_output_aliases={0: 0, 1: 1},
-        limit=63,
+        limit=62.25,
     )
     recv = lax.ppermute(send, "core", [(0, 1), (1, 0)])
 
@@ -331,49 +325,60 @@
         return lax.ppermute(value, inner, [(i, i ^ flip) for i in range(4)])
 
     block_rows = 16 * rows
-    blocks = [along(kv0, flip) for flip in FLIPS]
+    kv_far = along(kv0, 2)
+    kv_a = along(kv0, 1)
+    kv_b = along(kv0, 3)
     dq_shape = jax.ShapeDtypeStruct((2, 2, QR, HD), f32)
     part_shape = jax.ShapeDtypeStruct((block_rows, 4 * HD), bf16)
     options = dict(compiler_params=PARAMS)
-    dq, grads, far = pl.pallas_call(
+    dq, part0 = pl.pallas_call(
         first_kernel,
-        out_shape=(dq_shape, jax.ShapeDtypeStruct((2, R, 4 * HD), bf16), part_shape),
+        out_shape=(dq_shape, jax.ShapeDtypeStruct((block_rows, 4 * HD), f32)),
         in_specs=[VMEM] * 3,
-        out_specs=(VMEM,) * 3,
-        cost_estimate=cost(R + block_rows),
-        name="own_keys_and_far_block",
+        out_specs=(VMEM,) * 2,
+        cost_estimate=cost(block_rows),
+        name="own_block",
         **options,
-    )(mine, recv, blocks[0])
-    far = along(far, FLIPS[0])
-    dq, near_a, near_b = pl.pallas_call(
-        middle_kernel,
-        out_shape=(dq_shape, part_shape, part_shape),
-        in_specs=[VMEM] * 5,
-        out_specs=(VMEM,) * 3,
-        input_output_aliases={4: 0},
-        cost_estimate=cost(2 * block_rows),
-        name="near_blocks",
-        **options,
-    )(mine, recv, blocks[1], blocks[2], dq)
-    near_a = along(near_a, FLIPS[1])
-    near_b = along(near_b, FLIPS[2])
+    )(mine, recv, kv0)
+
+    def middle(kvs, dq):
+        count = len(kvs)
+        return pl.pallas_call(
+            functools.partial(middle_kernel, count),
+            out_shape=(dq_shape,) + (part_shape,) * count,
+            in_specs=[VMEM] * (3 + count),
+            out_specs=(VMEM,) * (1 + count),
+            input_output_aliases={2 + count: 0},
+            cost_estimate=cost(count * block_rows),
+            name="other_blocks",
+            **options,
+        )(mine, recv, *kvs, dq)
+
+    dq, far = middle([kv_far], dq)
+    far = along(far, 2)
+    dq, near_a, near_b = middle([kv_a, kv_b], dq)
+    near_a = along(near_a, 1)
+    near_b = along(near_b, 3)
     narrow = jax.ShapeDtypeStruct((R, KVH * HD), bf16)
-    back, part0, full_dq, full_dk, full_dv = pl.pallas_call(
+    back, full_dq, full_dk, full_dv = pl.pallas_call(
         last_kernel,
         out_shape=(
             jax.ShapeDtypeStruct((R, 2 * QR + 4 * HD), bf16),
-            jax.ShapeDtypeStruct((block_rows, 4 * HD), f32),
             jax.ShapeDtypeStruct((R, H * HD), bf16),
             narrow,
             narrow,
         ),
-        in_specs=[SMEM] + [VMEM] * 5 + [ANY],
-        out_specs=(VMEM, VMEM, ANY, ANY, ANY),
-        scratch_shapes=[pltpu.VMEM((R, 2 * QR), bf16), pltpu.SemaphoreType.DMA((3,))],
-        cost_estimate=cost(block_rows),
-        name="own_block",
+        in_specs=[SMEM] + [VMEM] * 3 + [ANY],
+        out_specs=(VMEM, ANY, ANY, ANY),
+        scratch_shapes=[
+            pltpu.VMEM((R, 2 * QR), bf16),
+            pltpu.VMEM((R, 4 * HD), bf16),
+            pltpu.SemaphoreType.DMA((3,)),
+        ],
+        cost_estimate=cost(R),
+        name="own_keys",
         **options,
-    )(core[None], mine, recv, kv0, dq, grads, far)
+    )(core[None], mine, recv, dq, far)
     total, back = simple(
         sum_blocks_kernel,
         (part_shape, jax.ShapeDtypeStruct(back.shape, bf16)),

time: 102 us -> 102 us (level)
    pallas_call x1, Pallas kernels: 3.74 us -> 2.66 us  [body(): pl.pallas_call(last_kernel, out_shape=(jax.ShapeDtypeStruct((R, 2 * QR +...]
    ppermute x6, waiting for transfers between devices: 5.39 us -> 4.32 us  [along(): return lax.ppermute(value, inner, [(i, i ^ flip) for i in range(4)])]
    pallas_call x2 -> x3, Pallas kernels: 11.8 us -> 12.9 us  [the longest x2 9.84 us: middle(): pl.pallas_call(functools.partial(middle_kernel, count), out_shape=(dq_sha...]
where the time goes in v3:
time: 102 us; the launch traced here: 101 us
  starting transfers between devices  54.3 us (53%)
  Pallas kernels  25.5 us (25%)
  waiting for transfers between devices  17.1 us (17%)
  local copies, waits for them, and re-layouts  1.68 us (2%)
  between operations  1.48 us (1%)
    ppermute x6, starting transfers between devices, along(): return lax.ppermute(value, inner, [(i, i ^ flip) for i in range(4)])  19.1 us
    all_to_all x1, starting transfers between devices, body(): kv0 = lax.all_to_all(shards, outer, 0, 0, tiled=True)  12 us
    pallas_call x2, Pallas kernels, middle(): pl.pallas_call(functools.partial(middle_kernel, count), out_shape=(dq_sha...  9.84 us
    all_to_all x1, starting transfers between devices, body(): total = lax.all_to_all(total, ('yh', 'core'), 0, 0, tiled=True)  9.75 us
    all_to_all x1, waiting for transfers between devices, body(): total = lax.all_to_all(total, ('yh', 'core'), 0, 0, tiled=True)  7.87 us
    pallas_call x1, Pallas kernels, prep(): pl.pallas_call(prep_kernel, out_shape=(shape, shape), in_specs=[pl.BlockS...  5.55 us
    ppermute x1, starting transfers between devices, body(): recv = lax.ppermute(send, 'core', [(0, 1), (1, 0)])  5.22 us
    pallas_call x6, Pallas kernels, simple(): pl.pallas_call(kernel, out_shape=out_shape, in_specs=in_specs or [VMEM] *...  4.46 us
  transfers between devices with their start and end apart: 11, of which 5 were waited for; matrix products, arithmetic and copies ran while one was open for 1% of the time, Pallas kernels for 22%

profile of v3, /device:TPU:1, one launch (start us, length us, event | category | flops | bytes accessed | tf_op | source)
XLA Modules:
  0.0 100.7 jit_solution(10836280672257009536)
XLA Ops:
  0.6 1.5 %shards.1.order_by = bf16[256,512]{1,0:T(8,128)(2,1)} custom-call(s32[1]{0:T(128)} %bitcast.core, bf16[16,512]{1,0:T(8,128)(2,1)} %k.1, bf16[16,512]{1,0:T(8,128)(2,1)} %v.1), custom_call_target="tpu_custom_call" | custom-call | tf_op jit(solution)/shard_map/shards/pallas_call | solution.py:263
  2.1 12.0 %all-to-all-start = ((bf16[16,16,512]{2,1,0:T(8,128)(2,1)}), bf16[16,16,512]{2,1,0:T(8,128)(2,1)S(1)}, u32[]{:S(2)}, u32[]{:S(2)}) async-start(bf16[16,16,512]{2,1,0:T(8,128)(2,1)} %bitcast.21), calls=%async_computation | async-start | bytes 524288 | tf_op jit(solution)/shard_map/all_to_all | solution.py:299
  14.7 0.6 pad_add_fusion.info
  15.3 5.5 %prep.1 = (bf16[2,2352,128]{2,1,0:T(8,128)(2,1)}, bf16[2,2352,128]{2,1,0:T(8,128)(2,1)}) custom-call(s32[2]{0:T(128)} %pad_add_fusion.info, bf16[128,4096]{1,0:T(8,128)(2,1)} %bitcast.23, bf16[128,4096]{1,0:T(8,128)(2,1)} %bitcast.24, bf16[128,4096]{1,0:T(8,128)(2,1)} %bitcast.25, bf16[128,512]{1,0:T(8,128)(2,1)} %bitcast.26, bf16[128,512]{1,0:T(8,128)(2,1)} %bitcast.27, ...), custom_call_target="tpu_custom_call" | custom-call | flops 10000000 | bytes 8388608 | tf_op jit(solution)/shard_map/prep/pallas_call | solution.py:98
  20.9 0.0 copy-start
  20.9 1.5 %all-to-all-done = bf16[16,16,512]{2,1,0:T(8,128)(2,1)S(1)} async-done(((bf16[16,16,512]{2,1,0:T(8,128)(2,1)}), bf16[16,16,512]{2,1,0:T(8,128)(2,1)S(1)}, u32[]{:S(2)}, u32[]{:S(2)}) %all-to-all-start) | async-done | bytes 262176 | tf_op jit(solution)/shard_map/all_to_all | solution.py:299
  22.4 0.0 copy-start.1
  22.4 0.7 copy-done.1
  23.1 5.2 %collective-permute-start = (bf16[2,2352,128]{2,1,0:T(8,128)(2,1)}, bf16[2,2352,128]{2,1,0:T(8,128)(2,1)S(1)}, u32[]{:S(2)}, u32[]{:S(2)}) collective-permute-start(bf16[2,2352,128]{2,1,0:T(8,128)(2,1)} %get-tuple-element.29), channel_id=1, source_target_pairs={{0,64},{64,0},{1,65},{65,1},{2,66},{66,2},{3,67},{67,3},{4,68},{68... | collective-permute-start | bytes 3612680 | tf_op jit(solution)/shard_map/ppermute | solution.py:322
  28.3 4.7 %collective-permute-start.3 = (bf16[256,512]{1,0:T(8,128)(2,1)}, bf16[256,512]{1,0:T(8,128)(2,1)S(1)}, u32[]{:S(2)}, u32[]{:S(2)}) collective-permute-start(bf16[256,512]{1,0:T(8,128)(2,1)} %get-tuple-element.30.kv), channel_id=1, source_target_pairs={{0,32},{16,48},{32,0},{48,16},{1,33},{17,49},{33,1},{49,17},{2,34}... | collective-permute-start | bytes 786440 | tf_op jit(solution)/shard_map/ppermute | solution.py:325
  33.0 2.8 %collective-permute-start.2 = (bf16[256,512]{1,0:T(8,128)(2,1)}, bf16[256,512]{1,0:T(8,128)(2,1)S(1)}, u32[]{:S(2)}, u32[]{:S(2)}) collective-permute-start(bf16[256,512]{1,0:T(8,128)(2,1)} %get-tuple-element.30.kv), channel_id=1, source_target_pairs={{0,48},{16,32},{32,16},{48,0},{1,49},{17,33},{33,17},{49,1},{2,50}... | collective-permute-start | bytes 786440 | tf_op jit(solution)/shard_map/ppermute | solution.py:325
  35.8 1.9 %collective-permute-start.1 = (bf16[256,512]{1,0:T(8,128)(2,1)}, bf16[256,512]{1,0:T(8,128)(2,1)S(1)}, u32[]{:S(2)}, u32[]{:S(2)}) collective-permute-start(bf16[256,512]{1,0:T(8,128)(2,1)} %get-tuple-element.30.kv), channel_id=1, source_target_pairs={{0,16},{16,0},{32,48},{48,32},{1,17},{17,1},{33,49},{49,33},{2,18}... | collective-permute-start | bytes 786440 | tf_op jit(solution)/shard_map/ppermute | solution.py:325
  37.7 0.0 collective-permute-done.recv
  37.7 0.0 copy-done
  37.7 0.0 copy-start.2
  37.7 1.0 copy-done.2
  38.7 3.0 %own_block.1 = (f32[2,2,1024,128]{3,2,1,0:T(8,128)S(1)}, f32[256,512]{1,0:T(8,128)S(1)}) custom-call(bf16[2,2352,128]{2,1,0:T(8,128)(2,1)S(1)} %copy-done, bf16[2,2352,128]{2,1,0:T(8,128)(2,1)S(1)} %collective-permute-done.recv, bf16[256,512]{1,0:T(8,128)(2,1)S(1)} %copy-done.2), custom_call_target="tpu_custom_call" | custom-call | flops 1342177280 | bytes 8388608 | tf_op jit(solution)/shard_map/own_block/pallas_call | solution.py:334
  41.7 0.0 collective-permute-done.3.refs_0_
  41.7 3.5 %other_blocks.2 = (f32[2,2,1024,128]{3,2,1,0:T(8,128)S(1)}, bf16[256,512]{1,0:T(8,128)(2,1)S(1)}) custom-call(bf16[2,2352,128]{2,1,0:T(8,128)(2,1)S(1)} %copy-done, bf16[2,2352,128]{2,1,0:T(8,128)(2,1)S(1)} %collective-permute-done.recv, bf16[256,512]{1,0:T(8,128)(2,1)S(1)} %collective-permute-done.3.refs_0_, ...), custom_call_target="tpu_custom_call", output_to_operand_aliasing={{0}: (3, {})} | custom-call | flops 1342177280 | bytes 8388608 | tf_op jit(solution)/shard_map/other_blocks/pallas_call | solution.py:346
  45.2 5.1 %collective-permute-start.6 = (bf16[256,512]{1,0:T(8,128)(2,1)S(1)}, bf16[256,512]{1,0:T(8,128)(2,1)S(1)}, u32[]{:S(2)}, u32[]{:S(2)}) collective-permute-start(bf16[256,512]{1,0:T(8,128)(2,1)S(1)} %get-tuple-element.36), channel_id=1, source_target_pairs={{0,32},{16,48},{32,0},{48,16},{1,33},{17,49},{33,1},{49,17},{2,34}... | collective-permute-start | bytes 786440 | tf_op jit(solution)/shard_map/ppermute | solution.py:325
  50.3 0.0 collective-permute-done.2.refs_1_
  50.3 0.0 collective-permute-done.1.refs_0_
  50.3 6.3 %other_blocks.3 = (f32[2,2,1024,128]{3,2,1,0:T(8,128)S(1)}, bf16[256,512]{1,0:T(8,128)(2,1)S(1)}, bf16[256,512]{1,0:T(8,128)(2,1)S(1)}) custom-call(bf16[2,2352,128]{2,1,0:T(8,128)(2,1)S(1)} %copy-done, bf16[2,2352,128]{2,1,0:T(8,128)(2,1)S(1)} %collective-permute-done.recv, ...), custom_call_target="tpu_custom_call", output_to_operand_aliasing={{0}: (4, {})} | custom-call | flops 2684354560 | bytes 8388608 | tf_op jit(solution)/shard_map/other_blocks/pallas_call | solution.py:346
  56.7 1.9 %collective-permute-start.4 = (bf16[256,512]{1,0:T(8,128)(2,1)S(1)}, bf16[256,512]{1,0:T(8,128)(2,1)S(1)}, u32[]{:S(2)}, u32[]{:S(2)}) collective-permute-start(bf16[256,512]{1,0:T(8,128)(2,1)S(1)} %get-tuple-element.34), channel_id=1, source_target_pairs={{0,16},{16,0},{32,48},{48,32},{1,17},{17,1},{33,49},{49,33},{2,18}... | collective-permute-start | bytes 786440 | tf_op jit(solution)/shard_map/ppermute | solution.py:325
  58.6 2.8 %collective-permute-start.5 = (bf16[256,512]{1,0:T(8,128)(2,1)S(1)}, bf16[256,512]{1,0:T(8,128)(2,1)S(1)}, u32[]{:S(2)}, u32[]{:S(2)}) collective-permute-start(bf16[256,512]{1,0:T(8,128)(2,1)S(1)} %get-tuple-element.35), channel_id=1, source_target_pairs={{0,48},{16,32},{32,16},{48,0},{1,49},{17,33},{33,17},{49,1},{2,50}... | collective-permute-start | bytes 786440 | tf_op jit(solution)/shard_map/ppermute | solution.py:325
  61.4 0.0 collective-permute-done.6.order_by.d
  61.4 2.7 %own_keys.1 = (bf16[128,2560]{1,0:T(8,128)(2,1)S(1)}, bf16[128,4096]{1,0:T(8,128)(2,1)}, bf16[128,512]{1,0:T(8,128)(2,1)}, bf16[128,512]{1,0:T(8,128)(2,1)}) custom-call(s32[1]{0:T(128)} %bitcast.core, bf16[2,2352,128]{2,1,0:T(8,128)(2,1)S(1)} %copy-done, bf16[2,2352,128]{2,1,0:T(8,128)(2,1)S(1)} %collective-permute-done.recv, ...), custom_call_target="tpu_custom_call" | custom-call | flops 671088640 | bytes 8388608 | tf_op jit(solution)/shard_map/own_keys/pallas_call | solution.py:363
  64.1 1.2 %collective-permute-done.4.b = bf16[256,512]{1,0:T(8,128)(2,1)S(1)} collective-permute-done((bf16[256,512]{1,0:T(8,128)(2,1)S(1)}, bf16[256,512]{1,0:T(8,128)(2,1)S(1)}, u32[]{:S(2)}, u32[]{:S(2)}) %collective-permute-start.4) | collective-permute-done | bytes 262176 | tf_op jit(solution)/shard_map/ppermute | solution.py:325
  65.2 3.1 %collective-permute-done.5.c = bf16[256,512]{1,0:T(8,128)(2,1)S(1)} collective-permute-done((bf16[256,512]{1,0:T(8,128)(2,1)S(1)}, bf16[256,512]{1,0:T(8,128)(2,1)S(1)}, u32[]{:S(2)}, u32[]{:S(2)}) %collective-permute-start.5) | collective-permute-done | bytes 262176 | tf_op jit(solution)/shard_map/ppermute | solution.py:325
  68.4 0.8 sum_blocks.1
  69.2 4.0 %all-to-all-start.1 = ((bf16[16,16,512]{2,1,0:T(8,128)(2,1)}), bf16[16,16,512]{2,1,0:T(8,128)(2,1)S(1)}, u32[]{:S(2)}, u32[]{:S(2)}) async-start(bf16[16,16,512]{2,1,0:T(8,128)(2,1)} %bitcast.13), calls=%async_computation.1 | async-start | bytes 524288 | tf_op jit(solution)/shard_map/all_to_all | solution.py:396
  73.2 4.2 %collective-permute-start.7 = (bf16[128,2560]{1,0:T(8,128)(2,1)S(1)}, bf16[128,2560]{1,0:T(8,128)(2,1)S(1)}, u32[]{:S(2)}, u32[]{:S(2)}) collective-permute-start(bf16[128,2560]{1,0:T(8,128)(2,1)S(1)} %get-tuple-element.39), channel_id=1, source_target_pairs={{0,64},{64,0},{1,65},{65,1},{2,66},{66,2},{3,67},{67,3},{4,68},{68... | collective-permute-start | bytes 1966088 | tf_op jit(solution)/shard_map/ppermute | solution.py:395
  77.4 3.4 %all-to-all-done.1 = bf16[16,16,512]{2,1,0:T(8,128)(2,1)S(1)} async-done(((bf16[16,16,512]{2,1,0:T(8,128)(2,1)}), bf16[16,16,512]{2,1,0:T(8,128)(2,1)S(1)}, u32[]{:S(2)}, u32[]{:S(2)}) %all-to-all-start.1) | async-done | bytes 262176 | tf_op jit(solution)/shard_map/all_to_all | solution.py:396
  80.9 0.7 sum_copies.1
  81.5 9.8 %all-to-all-start.2 = ((bf16[8,16,512]{2,1,0:T(8,128)(2,1)}), bf16[8,16,512]{2,1,0:T(8,128)(2,1)S(1)}, u32[]{:S(2)}, u32[]{:S(2)}) async-start(bf16[8,16,512]{2,1,0:T(8,128)(2,1)} %bitcast.15), calls=%async_computation.2 | async-start | bytes 262144 | tf_op jit(solution)/shard_map/all_to_all | solution.py:400
  91.3 0.0 collective-permute-done.7.got
  91.3 0.8 join.1
  92.2 7.9 %all-to-all-done.2 = bf16[8,16,512]{2,1,0:T(8,128)(2,1)S(1)} async-done(((bf16[8,16,512]{2,1,0:T(8,128)(2,1)}), bf16[8,16,512]{2,1,0:T(8,128)(2,1)S(1)}, u32[]{:S(2)}, u32[]{:S(2)}) %all-to-all-start.2) | async-done | bytes 131104 | tf_op jit(solution)/shard_map/all_to_all | solution.py:400
  100.0 0.6 sum_samples.1
  (1 shorter events, 0.0 us)
Async XLA Ops:
  2.1 20.3 %all-to-all-start = ((bf16[16,16,512]{2,1,0:T(8,128)(2,1)}), bf16[16,16,512]{2,1,0:T(8,128)(2,1)S(1)}, u32[]{:S(2)}, u32[]{:S(2)}) async-start(bf16[16,16,512]{2,1,0:T(8,128)(2,1)} %bitcast.21), calls=%async_computation | async-start | bytes 524288 | tf_op jit(solution)/shard_map/all_to_all | solution.py:299
  20.9 16.8 %copy-start = (bf16[2,2352,128]{2,1,0:T(8,128)(2,1)S(1)}, bf16[2,2352,128]{2,1,0:T(8,128)(2,1)}, u32[]{:S(2)}) copy-start(bf16[2,2352,128]{2,1,0:T(8,128)(2,1)} %get-tuple-element.27.mine) | copy-start | bytes 3612676
  22.4 0.7 copy-start.1
  23.1 14.6 %collective-permute-start = (bf16[2,2352,128]{2,1,0:T(8,128)(2,1)}, bf16[2,2352,128]{2,1,0:T(8,128)(2,1)S(1)}, u32[]{:S(2)}, u32[]{:S(2)}) collective-permute-start(bf16[2,2352,128]{2,1,0:T(8,128)(2,1)} %get-tuple-element.29), channel_id=1, source_target_pairs={{0,64},{64,0},{1,65},{65,1},{2,66},{66,2},{3,67},{67,3},{4,68},{68... | collective-permute-start | bytes 3612680 | tf_op jit(solution)/shard_map/ppermute | solution.py:322
  28.3 13.4 %collective-permute-start.3 = (bf16[256,512]{1,0:T(8,128)(2,1)}, bf16[256,512]{1,0:T(8,128)(2,1)S(1)}, u32[]{:S(2)}, u32[]{:S(2)}) collective-permute-start(bf16[256,512]{1,0:T(8,128)(2,1)} %get-tuple-element.30.kv), channel_id=1, source_target_pairs={{0,32},{16,48},{32,0},{48,16},{1,33},{17,49},{33,1},{49,17},{2,34}... | collective-permute-start | bytes 786440 | tf_op jit(solution)/shard_map/ppermute | solution.py:325
  33.0 17.3 %collective-permute-start.2 = (bf16[256,512]{1,0:T(8,128)(2,1)}, bf16[256,512]{1,0:T(8,128)(2,1)S(1)}, u32[]{:S(2)}, u32[]{:S(2)}) collective-permute-start(bf16[256,512]{1,0:T(8,128)(2,1)} %get-tuple-element.30.kv), channel_id=1, source_target_pairs={{0,48},{16,32},{32,16},{48,0},{1,49},{17,33},{33,17},{49,1},{2,50}... | collective-permute-start | bytes 786440 | tf_op jit(solution)/shard_map/ppermute | solution.py:325
  35.8 14.6 %collective-permute-start.1 = (bf16[256,512]{1,0:T(8,128)(2,1)}, bf16[256,512]{1,0:T(8,128)(2,1)S(1)}, u32[]{:S(2)}, u32[]{:S(2)}) collective-permute-start(bf16[256,512]{1,0:T(8,128)(2,1)} %get-tuple-element.30.kv), channel_id=1, source_target_pairs={{0,16},{16,0},{32,48},{48,32},{1,17},{17,1},{33,49},{49,33},{2,18}... | collective-permute-start | bytes 786440 | tf_op jit(solution)/shard_map/ppermute | solution.py:325
  37.7 1.0 copy-start.2
  45.2 16.2 %collective-permute-start.6 = (bf16[256,512]{1,0:T(8,128)(2,1)S(1)}, bf16[256,512]{1,0:T(8,128)(2,1)S(1)}, u32[]{:S(2)}, u32[]{:S(2)}) collective-permute-start(bf16[256,512]{1,0:T(8,128)(2,1)S(1)} %get-tuple-element.36), channel_id=1, source_target_pairs={{0,32},{16,48},{32,0},{48,16},{1,33},{17,49},{33,1},{49,17},{2,34}... | collective-permute-start | bytes 786440 | tf_op jit(solution)/shard_map/ppermute | solution.py:325
  56.7 8.6 %collective-permute-start.4 = (bf16[256,512]{1,0:T(8,128)(2,1)S(1)}, bf16[256,512]{1,0:T(8,128)(2,1)S(1)}, u32[]{:S(2)}, u32[]{:S(2)}) collective-permute-start(bf16[256,512]{1,0:T(8,128)(2,1)S(1)} %get-tuple-element.34), channel_id=1, source_target_pairs={{0,16},{16,0},{32,48},{48,32},{1,17},{17,1},{33,49},{49,33},{2,18}... | collective-permute-start | bytes 786440 | tf_op jit(solution)/shard_map/ppermute | solution.py:325
  58.6 9.8 %collective-permute-start.5 = (bf16[256,512]{1,0:T(8,128)(2,1)S(1)}, bf16[256,512]{1,0:T(8,128)(2,1)S(1)}, u32[]{:S(2)}, u32[]{:S(2)}) collective-permute-start(bf16[256,512]{1,0:T(8,128)(2,1)S(1)} %get-tuple-element.35), channel_id=1, source_target_pairs={{0,48},{16,32},{32,16},{48,0},{1,49},{17,33},{33,17},{49,1},{2,50}... | collective-permute-start | bytes 786440 | tf_op jit(solution)/shard_map/ppermute | solution.py:325
  69.2 11.7 %all-to-all-start.1 = ((bf16[16,16,512]{2,1,0:T(8,128)(2,1)}), bf16[16,16,512]{2,1,0:T(8,128)(2,1)S(1)}, u32[]{:S(2)}, u32[]{:S(2)}) async-start(bf16[16,16,512]{2,1,0:T(8,128)(2,1)} %bitcast.13), calls=%async_computation.1 | async-start | bytes 524288 | tf_op jit(solution)/shard_map/all_to_all | solution.py:396
  73.2 18.1 %collective-permute-start.7 = (bf16[128,2560]{1,0:T(8,128)(2,1)S(1)}, bf16[128,2560]{1,0:T(8,128)(2,1)S(1)}, u32[]{:S(2)}, u32[]{:S(2)}) collective-permute-start(bf16[128,2560]{1,0:T(8,128)(2,1)S(1)} %get-tuple-element.39), channel_id=1, source_target_pairs={{0,64},{64,0},{1,65},{65,1},{2,66},{66,2},{3,67},{67,3},{4,68},{68... | collective-permute-start | bytes 1966088 | tf_op jit(solution)/shard_map/ppermute | solution.py:395
  81.5 18.5 %all-to-all-start.2 = ((bf16[8,16,512]{2,1,0:T(8,128)(2,1)}), bf16[8,16,512]{2,1,0:T(8,128)(2,1)S(1)}, u32[]{:S(2)}, u32[]{:S(2)}) async-start(bf16[8,16,512]{2,1,0:T(8,128)(2,1)} %bitcast.15), calls=%async_computation.2 | async-start | bytes 262144 | tf_op jit(solution)/shard_map/all_to_all | solution.py:400

commit v4 on v3

--- a/solution.py
+++ b/solution.py
@@ -32,6 +32,7 @@
 VMEM = pl.BlockSpec(memory_space=pltpu.VMEM)
 SMEM = pl.BlockSpec(memory_space=pltpu.SMEM)
 ANY = pl.BlockSpec(memory_space=pl.ANY)
+FLIPS = (2, 1, 3)
 CHUNK = 512
 
 
@@ -159,19 +160,22 @@
     prompt_block(mine, recv, kv, emit_dq, out)
 
 
-def middle_kernel(count, mine, recv, *refs):
-    kvs, dq_in, dq, outs = refs[:count], refs[count], refs[count + 1], refs[count + 2 :]
-    for i, (kv, out) in enumerate(zip(kvs, outs)):
-
-        def emit_dq(r, g, cs, value):
-            source = dq if i else dq_in
-            dq[r, g, cs, :] = source[r, g, cs, :] + value
-
-        prompt_block(mine, recv, kv, emit_dq, out)
-
-
-def last_kernel(core, mine, recv, dq_in, order_by, back, full_dq, full_dk, full_dv, own, grads, sems):
+def middle_kernel(mine, recv, kv_a, kv_b, dq_in, dq, out_a, out_b):
+    def emit_a(r, g, cs, value):
+        dq[r, g, cs, :] = dq_in[r, g, cs, :] + value
+
+    def emit_b(r, g, cs, value):
+        dq[r, g, cs, :] += value
+
+    prompt_block(mine, recv, kv_a, emit_a, out_a)
+    prompt_block(mine, recv, kv_b, emit_b, out_b)
+
+
+def last_kernel(core, mine, recv, kv, dq_in, order_by, back, out, full_dq, full_dk, full_dv, dq, own, grads, sems):
     half = 2 * HD
+
+    def emit_block(r, g, cs, value):
+        dq[r, g, cs, :] = dq_in[r, g, cs, :] + value
 
     def place(full, width):
         return full.at[:, pl.ds(pl.multiple_of(core[0] * width, width), width)]
@@ -181,6 +185,7 @@
         pltpu.make_async_copy(grads.at[:, :half], place(full_dk, half), sems.at[1]),
         pltpu.make_async_copy(grads.at[:, half:], place(full_dv, half), sems.at[2]),
     ]
+    prompt_block(mine, recv, kv, emit_block, out)
     for r, (ref, target) in enumerate(((mine, own), (recv, back))):
         dest, base = (grads, 0) if r == 0 else (back, 2 * QR)
         for g in range(2):
@@ -192,7 +197,7 @@
                 dk_c, dv_c, dq_c, cs = tile_grads(ref, g, chunk, keys, values, True)
                 dk += dk_c
                 dv += dv_c
-                total = ((dq_in[r, g, cs, :] + dq_c) * SCALE).astype(bf16)
+                total = ((dq[r, g, cs, :] + dq_c) * SCALE).astype(bf16)
                 for j in range(CHUNK // R):
                     h = g * G + chunk * (CHUNK // R) + j
                     target[:, h * HD : (h + 1) * HD] = total[j * R : (j + 1) * R, :]
@@ -325,68 +330,62 @@
         return lax.ppermute(value, inner, [(i, i ^ flip) for i in range(4)])
 
     block_rows = 16 * rows
-    kv_far = along(kv0, 2)
-    kv_a = along(kv0, 1)
-    kv_b = along(kv0, 3)
+    blocks = [along(kv0, flip) for flip in FLIPS]
     dq_shape = jax.ShapeDtypeStruct((2, 2, QR, HD), f32)
     part_shape = jax.ShapeDtypeStruct((block_rows, 4 * HD), bf16)
     options = dict(compiler_params=PARAMS)
-    dq, part0 = pl.pallas_call(
+    dq, part1 = pl.pallas_call(
         first_kernel,
-        out_shape=(dq_shape, jax.ShapeDtypeStruct((block_rows, 4 * HD), f32)),
+        out_shape=(dq_shape, part_shape),
         in_specs=[VMEM] * 3,
         out_specs=(VMEM,) * 2,
         cost_estimate=cost(block_rows),
-        name="own_block",
+        name="far_block",
         **options,
-    )(mine, recv, kv0)
-
-    def middle(kvs, dq):
-        count = len(kvs)
-        return pl.pallas_call(
-            functools.partial(middle_kernel, count),
-            out_shape=(dq_shape,) + (part_shape,) * count,
-            in_specs=[VMEM] * (3 + count),
-            out_specs=(VMEM,) * (1 + count),
-            input_output_aliases={2 + count: 0},
-            cost_estimate=cost(count * block_rows),
-            name="other_blocks",
-            **options,
-        )(mine, recv, *kvs, dq)
-
-    dq, far = middle([kv_far], dq)
-    far = along(far, 2)
-    dq, near_a, near_b = middle([kv_a, kv_b], dq)
-    near_a = along(near_a, 1)
-    near_b = along(near_b, 3)
+    )(mine, recv, blocks[0])
+    part1 = along(part1, FLIPS[0])
+    dq, part2, part3 = pl.pallas_call(
+        middle_kernel,
+        out_shape=(dq_shape, part_shape, part_shape),
+        in_specs=[VMEM] * 5,
+        out_specs=(VMEM,) * 3,
+        input_output_aliases={4: 0},
+        cost_estimate=cost(2 * block_rows),
+        name="near_blocks",
+        **options,
+    )(mine, recv, blocks[1], blocks[2], dq)
+    part2 = along(part2, FLIPS[1])
+    part3 = along(part3, FLIPS[2])
     narrow = jax.ShapeDtypeStruct((R, KVH * HD), bf16)
-    back, full_dq, full_dk, full_dv = pl.pallas_call(
+    back, part0, full_dq, full_dk, full_dv = pl.pallas_call(
         last_kernel,
         out_shape=(
             jax.ShapeDtypeStruct((R, 2 * QR + 4 * HD), bf16),
+            jax.ShapeDtypeStruct((block_rows, 4 * HD), f32),
             jax.ShapeDtypeStruct((R, H * HD), bf16),
             narrow,
             narrow,
         ),
-        in_specs=[SMEM] + [VMEM] * 3 + [ANY],
-        out_specs=(VMEM, ANY, ANY, ANY),
+        in_specs=[SMEM] + [VMEM] * 4 + [ANY],
+        out_specs=(VMEM, VMEM, ANY, ANY, ANY),
         scratch_shapes=[
+            pltpu.VMEM((2, 2, QR, HD), f32),
             pltpu.VMEM((R, 2 * QR), bf16),
             pltpu.VMEM((R, 4 * HD), bf16),
             pltpu.SemaphoreType.DMA((3,)),
         ],
-        cost_estimate=cost(R),
-        name="own_keys",
+        cost_estimate=cost(block_rows + R),
+        name="own_block_and_own_keys",
         **options,
-    )(core[None], mine, recv, dq, far)
+    )(core[None], mine, recv, kv0, dq, part1)
     total, back = simple(
         sum_blocks_kernel,
         (part_shape, jax.ShapeDtypeStruct(back.shape, bf16)),
         "sum_blocks",
         part0,
-        near_a,
-        near_b,
-        far,
+        part1,
+        part3,
+        part2,
         back,
         in_specs=[VMEM] * 4 + [ANY],
         out_specs=(VMEM, ANY),

time: 102 us -> 98 us (0.961)
  waiting for transfers between devices: 17.1 us -> 14.3 us
    pallas_call x3 -> x2, Pallas kernels: 12.9 us -> 9.37 us  [the longest x1 6.35 us: body(): pl.pallas_call(middle_kernel, out_shape=(dq_shape, part_shape, part_shape...]
    pallas_call x1, Pallas kernels: 2.66 us -> 5.87 us  [body(): pl.pallas_call(last_kernel, out_shape=(jax.ShapeDtypeStruct((R, 2 * QR +...]
    ppermute x6, waiting for transfers between devices: 4.32 us -> 2.44 us  [along(): return lax.ppermute(value, inner, [(i, i ^ flip) for i in range(4)])]
  transfers between devices with their start and end apart: 11 -> 11, of which waited for: 5 -> 5; matrix products, arithmetic and copies ran while one was open for 1% -> 1% of each run, Pallas kernels for 22% -> 23%
where the time goes in v4:
time: 98 us; the launch traced here: 96.9 us
  starting transfers between devices  54.6 us (56%)
  Pallas kernels  25.3 us (26%)
  waiting for transfers between devices  14.3 us (15%)
  between operations  1.47 us (2%)
    ppermute x6, starting transfers between devices, along(): return lax.ppermute(value, inner, [(i, i ^ flip) for i in range(4)])  18.9 us
    all_to_all x1, starting transfers between devices, body(): kv0 = lax.all_to_all(shards, outer, 0, 0, tiled=True)  12 us
    all_to_all x1, starting transfers between devices, body(): total = lax.all_to_all(total, ('yh', 'core'), 0, 0, tiled=True)  10 us
    all_to_all x1, waiting for transfers between devices, body(): total = lax.all_to_all(total, ('yh', 'core'), 0, 0, tiled=True)  7.19 us
    pallas_call x1, Pallas kernels, body(): pl.pallas_call(middle_kernel, out_shape=(dq_shape, part_shape, part_shape...  6.35 us
    pallas_call x1, Pallas kernels, body(): pl.pallas_call(last_kernel, out_shape=(jax.ShapeDtypeStruct((R, 2 * QR +...  5.87 us
    pallas_call x1, Pallas kernels, prep(): pl.pallas_call(prep_kernel, out_shape=(shape, shape), in_specs=[pl.BlockS...  5.55 us
    ppermute x1, starting transfers between devices, body(): recv = lax.ppermute(send, 'core', [(0, 1), (1, 0)])  5.22 us
  transfers between devices with their start and end apart: 11, of which 5 were waited for; matrix products, arithmetic and copies ran while one was open for 1% of the time, Pallas kernels for 23%

profile of v4, /device:TPU:1, one launch (start us, length us, event | category | flops | bytes accessed | tf_op | source)
XLA Modules:
  0.0 96.9 jit_solution(1409623099083386427)
XLA Ops:
  0.6 1.5 %shards.1.order_by = bf16[256,512]{1,0:T(8,128)(2,1)} custom-call(s32[1]{0:T(128)} %bitcast.core, bf16[16,512]{1,0:T(8,128)(2,1)} %k.1, bf16[16,512]{1,0:T(8,128)(2,1)} %v.1), custom_call_target="tpu_custom_call" | custom-call | tf_op jit(solution)/shard_map/shards/pallas_call | solution.py:268
  2.1 12.0 %all-to-all-start = ((bf16[16,16,512]{2,1,0:T(8,128)(2,1)}), bf16[16,16,512]{2,1,0:T(8,128)(2,1)S(1)}, u32[]{:S(2)}, u32[]{:S(2)}) async-start(bf16[16,16,512]{2,1,0:T(8,128)(2,1)} %bitcast.21), calls=%async_computation | async-start | bytes 524288 | tf_op jit(solution)/shard_map/all_to_all | solution.py:304
  14.7 0.6 pad_add_fusion.info
  15.3 5.6 %prep.1 = (bf16[2,2352,128]{2,1,0:T(8,128)(2,1)}, bf16[2,2352,128]{2,1,0:T(8,128)(2,1)}) custom-call(s32[2]{0:T(128)} %pad_add_fusion.info, bf16[128,4096]{1,0:T(8,128)(2,1)} %bitcast.23, bf16[128,4096]{1,0:T(8,128)(2,1)} %bitcast.24, bf16[128,4096]{1,0:T(8,128)(2,1)} %bitcast.25, bf16[128,512]{1,0:T(8,128)(2,1)} %bitcast.26, bf16[128,512]{1,0:T(8,128)(2,1)} %bitcast.27, ...), custom_call_target="tpu_custom_call" | custom-call | flops 10000000 | bytes 8388608 | tf_op jit(solution)/shard_map/prep/pallas_call | solution.py:99
  20.9 0.0 copy-start.2
  20.9 1.5 %all-to-all-done = bf16[16,16,512]{2,1,0:T(8,128)(2,1)S(1)} async-done(((bf16[16,16,512]{2,1,0:T(8,128)(2,1)}), bf16[16,16,512]{2,1,0:T(8,128)(2,1)S(1)}, u32[]{:S(2)}, u32[]{:S(2)}) %all-to-all-start) | async-done | bytes 262176 | tf_op jit(solution)/shard_map/all_to_all | solution.py:304
  22.4 0.0 copy-start
  22.4 0.7 copy-done
  23.1 5.2 %collective-permute-start = (bf16[2,2352,128]{2,1,0:T(8,128)(2,1)}, bf16[2,2352,128]{2,1,0:T(8,128)(2,1)S(1)}, u32[]{:S(2)}, u32[]{:S(2)}) collective-permute-start(bf16[2,2352,128]{2,1,0:T(8,128)(2,1)} %get-tuple-element.28), channel_id=1, source_target_pairs={{0,64},{64,0},{1,65},{65,1},{2,66},{66,2},{3,67},{67,3},{4,68},{68... | collective-permute-start | bytes 3612680 | tf_op jit(solution)/shard_map/ppermute | solution.py:327
  28.3 4.7 %collective-permute-start.3 = (bf16[256,512]{1,0:T(8,128)(2,1)}, bf16[256,512]{1,0:T(8,128)(2,1)S(1)}, u32[]{:S(2)}, u32[]{:S(2)}) collective-permute-start(bf16[256,512]{1,0:T(8,128)(2,1)} %get-tuple-element.29.kv), channel_id=1, source_target_pairs={{0,32},{16,48},{32,0},{48,16},{1,33},{17,49},{33,1},{49,17},{2,34}... | collective-permute-start | bytes 786440 | tf_op jit(solution)/shard_map/ppermute | solution.py:330
  33.0 2.8 %collective-permute-start.2 = (bf16[256,512]{1,0:T(8,128)(2,1)}, bf16[256,512]{1,0:T(8,128)(2,1)S(1)}, u32[]{:S(2)}, u32[]{:S(2)}) collective-permute-start(bf16[256,512]{1,0:T(8,128)(2,1)} %get-tuple-element.29.kv), channel_id=1, source_target_pairs={{0,48},{16,32},{32,16},{48,0},{1,49},{17,33},{33,17},{49,1},{2,50}... | collective-permute-start | bytes 786440 | tf_op jit(solution)/shard_map/ppermute | solution.py:330
  35.8 1.9 %collective-permute-start.1 = (bf16[256,512]{1,0:T(8,128)(2,1)}, bf16[256,512]{1,0:T(8,128)(2,1)S(1)}, u32[]{:S(2)}, u32[]{:S(2)}) collective-permute-start(bf16[256,512]{1,0:T(8,128)(2,1)} %get-tuple-element.29.kv), channel_id=1, source_target_pairs={{0,16},{16,0},{32,48},{48,32},{1,17},{17,1},{33,49},{49,33},{2,18}... | collective-permute-start | bytes 786440 | tf_op jit(solution)/shard_map/ppermute | solution.py:330
  37.7 2.2 %collective-permute-done.3.kv = bf16[256,512]{1,0:T(8,128)(2,1)S(1)} collective-permute-done((bf16[256,512]{1,0:T(8,128)(2,1)}, bf16[256,512]{1,0:T(8,128)(2,1)S(1)}, u32[]{:S(2)}, u32[]{:S(2)}) %collective-permute-start.3) | collective-permute-done | bytes 262176 | tf_op jit(solution)/shard_map/ppermute | solution.py:330
  39.9 0.0 collective-permute-done.recv
  39.9 0.0 copy-done.2
  39.9 3.0 %far_block.1 = (f32[2,2,1024,128]{3,2,1,0:T(8,128)S(1)}, bf16[256,512]{1,0:T(8,128)(2,1)S(1)}) custom-call(bf16[2,2352,128]{2,1,0:T(8,128)(2,1)S(1)} %copy-done.2, bf16[2,2352,128]{2,1,0:T(8,128)(2,1)S(1)} %collective-permute-done.recv, bf16[256,512]{1,0:T(8,128)(2,1)S(1)} %collective-permute-done.3.kv), custom_call_target="tpu_custom_call" | custom-call | flops 1342177280 | bytes 8388608 | tf_op jit(solution)/shard_map/far_block/pallas_call | solution.py:337
  42.9 4.7 %collective-permute-start.4 = (bf16[256,512]{1,0:T(8,128)(2,1)S(1)}, bf16[256,512]{1,0:T(8,128)(2,1)S(1)}, u32[]{:S(2)}, u32[]{:S(2)}) collective-permute-start(bf16[256,512]{1,0:T(8,128)(2,1)S(1)} %get-tuple-element.32), channel_id=1, source_target_pairs={{0,32},{16,48},{32,0},{48,16},{1,33},{17,49},{33,1},{49,17},{2,34}... | collective-permute-start | bytes 786440 | tf_op jit(solution)/shard_map/ppermute | solution.py:330
  47.6 0.0 collective-permute-done.2.kv_b
  47.6 0.0 collective-permute-done.1.kv_a
  47.6 0.0 copy-start.1
  47.6 6.4 %near_blocks.1 = (f32[2,2,1024,128]{3,2,1,0:T(8,128)S(1)}, bf16[256,512]{1,0:T(8,128)(2,1)S(1)}, bf16[256,512]{1,0:T(8,128)(2,1)S(1)}) custom-call(bf16[2,2352,128]{2,1,0:T(8,128)(2,1)S(1)} %copy-done.2, bf16[2,2352,128]{2,1,0:T(8,128)(2,1)S(1)} %collective-permute-done.recv, ...), custom_call_target="tpu_custom_call", output_to_operand_aliasing={{0}: (4, {})} | custom-call | flops 2684354560 | bytes 8388608 | tf_op jit(solution)/shard_map/near_blocks/pallas_call | solution.py:347
  54.0 2.8 %collective-permute-start.5 = (bf16[256,512]{1,0:T(8,128)(2,1)S(1)}, bf16[256,512]{1,0:T(8,128)(2,1)S(1)}, u32[]{:S(2)}, u32[]{:S(2)}) collective-permute-start(bf16[256,512]{1,0:T(8,128)(2,1)S(1)} %get-tuple-element.34), channel_id=1, source_target_pairs={{0,48},{16,32},{32,16},{48,0},{1,49},{17,33},{33,17},{49,1},{2,50}... | collective-permute-start | bytes 786440 | tf_op jit(solution)/shard_map/ppermute | solution.py:330
  56.8 2.1 %collective-permute-start.6 = (bf16[256,512]{1,0:T(8,128)(2,1)S(1)}, bf16[256,512]{1,0:T(8,128)(2,1)S(1)}, u32[]{:S(2)}, u32[]{:S(2)}) collective-permute-start(bf16[256,512]{1,0:T(8,128)(2,1)S(1)} %get-tuple-element.35), channel_id=1, source_target_pairs={{0,16},{16,0},{32,48},{48,32},{1,17},{17,1},{33,49},{49,33},{2,18}... | collective-permute-start | bytes 786440 | tf_op jit(solution)/shard_map/ppermute | solution.py:330
  58.9 0.0 collective-permute-done.4.order_by.b
  58.9 0.0 copy-done.1
  58.9 5.9 %own_block_and_own_keys.1 = (bf16[128,2560]{1,0:T(8,128)(2,1)S(1)}, f32[256,512]{1,0:T(8,128)S(1)}, bf16[128,4096]{1,0:T(8,128)(2,1)}, bf16[128,512]{1,0:T(8,128)(2,1)}, bf16[128,512]{1,0:T(8,128)(2,1)}) custom-call(s32[1]{0:T(128)} %bitcast.core, bf16[2,2352,128]{2,1,0:T(8,128)(2,1)S(1)} %copy-done.2, bf16[2,2352,128]{2,1,0:T(8,128)(2,1)S(1)} %collective-permute-done.recv, ...), custom_call_target="tpu_custom_call" | custom-call | flops 2013265920 | bytes 8388608 | tf_op jit(solution)/shard_map/own_block_and_own_keys/pallas_call | solution.py:360
  64.8 0.0 collective-permute-done.5.c
  64.8 0.3 collective-permute-done.6.d
  65.0 0.8 sum_blocks.1
  65.9 4.0 %all-to-all-start.1 = ((bf16[16,16,512]{2,1,0:T(8,128)(2,1)}), bf16[16,16,512]{2,1,0:T(8,128)(2,1)S(1)}, u32[]{:S(2)}, u32[]{:S(2)}) async-start(bf16[16,16,512]{2,1,0:T(8,128)(2,1)} %bitcast.13), calls=%async_computation.1 | async-start | bytes 524288 | tf_op jit(solution)/shard_map/all_to_all | solution.py:395
  69.9 4.5 %collective-permute-start.7 = (bf16[128,2560]{1,0:T(8,128)(2,1)S(1)}, bf16[128,2560]{1,0:T(8,128)(2,1)S(1)}, u32[]{:S(2)}, u32[]{:S(2)}) collective-permute-start(bf16[128,2560]{1,0:T(8,128)(2,1)S(1)} %get-tuple-element.37), channel_id=1, source_target_pairs={{0,64},{64,0},{1,65},{65,1},{2,66},{66,2},{3,67},{67,3},{4,68},{68... | collective-permute-start | bytes 1966088 | tf_op jit(solution)/shard_map/ppermute | solution.py:394
  74.4 3.1 %all-to-all-done.1 = bf16[16,16,512]{2,1,0:T(8,128)(2,1)S(1)} async-done(((bf16[16,16,512]{2,1,0:T(8,128)(2,1)}), bf16[16,16,512]{2,1,0:T(8,128)(2,1)S(1)}, u32[]{:S(2)}, u32[]{:S(2)}) %all-to-all-start.1) | async-done | bytes 262176 | tf_op jit(solution)/shard_map/all_to_all | solution.py:395
  77.5 0.7 sum_copies.1
  78.2 10.0 %all-to-all-start.2 = ((bf16[8,16,512]{2,1,0:T(8,128)(2,1)}), bf16[8,16,512]{2,1,0:T(8,128)(2,1)S(1)}, u32[]{:S(2)}, u32[]{:S(2)}) async-start(bf16[8,16,512]{2,1,0:T(8,128)(2,1)} %bitcast.15), calls=%async_computation.2 | async-start | bytes 262144 | tf_op jit(solution)/shard_map/all_to_all | solution.py:399
  88.3 0.0 collective-permute-done.7.got
  88.3 0.8 join.1
  89.1 7.2 %all-to-all-done.2 = bf16[8,16,512]{2,1,0:T(8,128)(2,1)S(1)} async-done(((bf16[8,16,512]{2,1,0:T(8,128)(2,1)}), bf16[8,16,512]{2,1,0:T(8,128)(2,1)S(1)}, u32[]{:S(2)}, u32[]{:S(2)}) %all-to-all-start.2) | async-done | bytes 131104 | tf_op jit(solution)/shard_map/all_to_all | solution.py:399
  96.3 0.6 sum_samples.1
  (1 shorter events, 0.0 us)
Async XLA Ops:
  2.1 20.3 %all-to-all-start = ((bf16[16,16,512]{2,1,0:T(8,128)(2,1)}), bf16[16,16,512]{2,1,0:T(8,128)(2,1)S(1)}, u32[]{:S(2)}, u32[]{:S(2)}) async-start(bf16[16,16,512]{2,1,0:T(8,128)(2,1)} %bitcast.21), calls=%async_computation | async-start | bytes 524288 | tf_op jit(solution)/shard_map/all_to_all | solution.py:304
  20.9 19.0 %copy-start.2 = (bf16[2,2352,128]{2,1,0:T(8,128)(2,1)S(1)}, bf16[2,2352,128]{2,1,0:T(8,128)(2,1)}, u32[]{:S(2)}) copy-start(bf16[2,2352,128]{2,1,0:T(8,128)(2,1)} %get-tuple-element.26.mine) | copy-start | bytes 3612676
  22.4 0.7 copy-start
  23.1 16.8 %collective-permute-start = (bf16[2,2352,128]{2,1,0:T(8,128)(2,1)}, bf16[2,2352,128]{2,1,0:T(8,128)(2,1)S(1)}, u32[]{:S(2)}, u32[]{:S(2)}) collective-permute-start(bf16[2,2352,128]{2,1,0:T(8,128)(2,1)} %get-tuple-element.28), channel_id=1, source_target_pairs={{0,64},{64,0},{1,65},{65,1},{2,66},{66,2},{3,67},{67,3},{4,68},{68... | collective-permute-start | bytes 3612680 | tf_op jit(solution)/shard_map/ppermute | solution.py:327
  28.3 11.5 %collective-permute-start.3 = (bf16[256,512]{1,0:T(8,128)(2,1)}, bf16[256,512]{1,0:T(8,128)(2,1)S(1)}, u32[]{:S(2)}, u32[]{:S(2)}) collective-permute-start(bf16[256,512]{1,0:T(8,128)(2,1)} %get-tuple-element.29.kv), channel_id=1, source_target_pairs={{0,32},{16,48},{32,0},{48,16},{1,33},{17,49},{33,1},{49,17},{2,34}... | collective-permute-start | bytes 786440 | tf_op jit(solution)/shard_map/ppermute | solution.py:330
  33.0 14.6 %collective-permute-start.2 = (bf16[256,512]{1,0:T(8,128)(2,1)}, bf16[256,512]{1,0:T(8,128)(2,1)S(1)}, u32[]{:S(2)}, u32[]{:S(2)}) collective-permute-start(bf16[256,512]{1,0:T(8,128)(2,1)} %get-tuple-element.29.kv), channel_id=1, source_target_pairs={{0,48},{16,32},{32,16},{48,0},{1,49},{17,33},{33,17},{49,1},{2,50}... | collective-permute-start | bytes 786440 | tf_op jit(solution)/shard_map/ppermute | solution.py:330
  35.8 11.8 %collective-permute-start.1 = (bf16[256,512]{1,0:T(8,128)(2,1)}, bf16[256,512]{1,0:T(8,128)(2,1)S(1)}, u32[]{:S(2)}, u32[]{:S(2)}) collective-permute-start(bf16[256,512]{1,0:T(8,128)(2,1)} %get-tuple-element.29.kv), channel_id=1, source_target_pairs={{0,16},{16,0},{32,48},{48,32},{1,17},{17,1},{33,49},{49,33},{2,18}... | collective-permute-start | bytes 786440 | tf_op jit(solution)/shard_map/ppermute | solution.py:330
  42.9 16.0 %collective-permute-start.4 = (bf16[256,512]{1,0:T(8,128)(2,1)S(1)}, bf16[256,512]{1,0:T(8,128)(2,1)S(1)}, u32[]{:S(2)}, u32[]{:S(2)}) collective-permute-start(bf16[256,512]{1,0:T(8,128)(2,1)S(1)} %get-tuple-element.32), channel_id=1, source_target_pairs={{0,32},{16,48},{32,0},{48,16},{1,33},{17,49},{33,1},{49,17},{2,34}... | collective-permute-start | bytes 786440 | tf_op jit(solution)/shard_map/ppermute | solution.py:330
  47.6 11.3 %copy-start.1 = (bf16[256,512]{1,0:T(8,128)(2,1)S(1)}, bf16[256,512]{1,0:T(8,128)(2,1)}, u32[]{:S(2)}) copy-start(bf16[256,512]{1,0:T(8,128)(2,1)} %get-tuple-element.29.kv) | copy-start | bytes 786436
  54.0 10.8 %collective-permute-start.5 = (bf16[256,512]{1,0:T(8,128)(2,1)S(1)}, bf16[256,512]{1,0:T(8,128)(2,1)S(1)}, u32[]{:S(2)}, u32[]{:S(2)}) collective-permute-start(bf16[256,512]{1,0:T(8,128)(2,1)S(1)} %get-tuple-element.34), channel_id=1, source_target_pairs={{0,48},{16,32},{32,16},{48,0},{1,49},{17,33},{33,17},{49,1},{2,50}... | collective-permute-start | bytes 786440 | tf_op jit(solution)/shard_map/ppermute | solution.py:330
  56.8 8.3 %collective-permute-start.6 = (bf16[256,512]{1,0:T(8,128)(2,1)S(1)}, bf16[256,512]{1,0:T(8,128)(2,1)S(1)}, u32[]{:S(2)}, u32[]{:S(2)}) collective-permute-start(bf16[256,512]{1,0:T(8,128)(2,1)S(1)} %get-tuple-element.35), channel_id=1, source_target_pairs={{0,16},{16,0},{32,48},{48,32},{1,17},{17,1},{33,49},{49,33},{2,18}... | collective-permute-start | bytes 786440 | tf_op jit(solution)/shard_map/ppermute | solution.py:330
  65.9 11.7 %all-to-all-start.1 = ((bf16[16,16,512]{2,1,0:T(8,128)(2,1)}), bf16[16,16,512]{2,1,0:T(8,128)(2,1)S(1)}, u32[]{:S(2)}, u32[]{:S(2)}) async-start(bf16[16,16,512]{2,1,0:T(8,128)(2,1)} %bitcast.13), calls=%async_computation.1 | async-start | bytes 524288 | tf_op jit(solution)/shard_map/all_to_all | solution.py:395
  69.9 18.4 %collective-permute-start.7 = (bf16[128,2560]{1,0:T(8,128)(2,1)S(1)}, bf16[128,2560]{1,0:T(8,128)(2,1)S(1)}, u32[]{:S(2)}, u32[]{:S(2)}) collective-permute-start(bf16[128,2560]{1,0:T(8,128)(2,1)S(1)} %get-tuple-element.37), channel_id=1, source_target_pairs={{0,64},{64,0},{1,65},{65,1},{2,66},{66,2},{3,67},{67,3},{4,68},{68... | collective-permute-start | bytes 1966088 | tf_op jit(solution)/shard_map/ppermute | solution.py:394
  78.2 18.1 %all-to-all-start.2 = ((bf16[8,16,512]{2,1,0:T(8,128)(2,1)}), bf16[8,16,512]{2,1,0:T(8,128)(2,1)S(1)}, u32[]{:S(2)}, u32[]{:S(2)}) async-start(bf16[8,16,512]{2,1,0:T(8,128)(2,1)} %bitcast.15), calls=%async_computation.2 | async-start | bytes 262144 | tf_op jit(solution)/shard_map/all_to_all | solution.py:399

commit v5 on v4

--- a/solution.py
+++ b/solution.py
@@ -48,9 +48,9 @@
     return hi, mid, low
 
 
-def prep_kernel(info, q, do, out, k, v, lse, order_by, send, mine, q_buf, do_buf, out_buf, k_buf, v_buf, sems, kv_sems):
-    core = info[0]
-    length = info[1]
+def prep_kernel(core_ref, length_ref, q, do, out, k, v, lse, order_by, send, mine, q_buf, do_buf, out_buf, k_buf, v_buf, sems, kv_sems):
+    core = core_ref[0]
+    length = length_ref[0]
     order = (2 * (1 - core), 2 * (1 - core) + 1, 2 * core, 2 * core + 1)
     wide = [
         [
@@ -99,13 +99,13 @@
     return pl.pallas_call(
         prep_kernel,
         out_shape=(shape, shape),
-        in_specs=[pl.BlockSpec(memory_space=pltpu.SMEM)] + [whole] * 5 + [VMEM, whole],
+        in_specs=[SMEM, SMEM] + [whole] * 5 + [VMEM, whole],
         out_specs=(VMEM, VMEM),
         scratch_shapes=[wide, wide, wide, narrow, narrow, pltpu.SemaphoreType.DMA((3, 4)), pltpu.SemaphoreType.DMA((2,))],
         compiler_params=pltpu.CompilerParams(vmem_limit_bytes=61 * 2**20),
         cost_estimate=pl.CostEstimate(flops=10**7, bytes_accessed=8 * 2**20, transcendentals=0),
         name="prep",
-    )(jnp.stack([core, length]), q, do, out, k, v, lse_t, order_by)
+    )(core[None], length, q, do, out, k, v, lse_t, order_by)
 
 
 def stat_row(ref, g, kind, first, count):
@@ -304,7 +304,7 @@
     kv0 = lax.all_to_all(shards, outer, 0, 0, tiled=True)
     send, mine = prep(
         core,
-        resp_lengths[0],
+        resp_lengths,
         resp_q[0],
         resp_do[0],
         resp_out[0],

time: 98 us -> 97.7 us (level)
  transfers between devices with their start and end apart: 11 -> 11, of which waited for: 5 -> 5; matrix products, arithmetic and copies ran while one was open for 1% -> 0% of each run, Pallas kernels for 23% -> 23%
where the time goes in v5:
time: 97.7 us; the launch traced here: 96.6 us
  starting transfers between devices  54.3 us (56%)
  Pallas kernels  25.3 us (26%)
  waiting for transfers between devices  14.8 us (15%)
  between operations  1.47 us (2%)
    ppermute x6, starting transfers between devices, along(): return lax.ppermute(value, inner, [(i, i ^ flip) for i in range(4)])  18.9 us
    all_to_all x1, starting transfers between devices, body(): kv0 = lax.all_to_all(shards, outer, 0, 0, tiled=True)  12 us
    all_to_all x1, starting transfers between devices, body(): total = lax.all_to_all(total, ('yh', 'core'), 0, 0, tiled=True)  10 us
    all_to_all x1, waiting for transfers between devices, body(): total = lax.all_to_all(total, ('yh', 'core'), 0, 0, tiled=True)  7.19 us
    pallas_call x1, Pallas kernels, body(): pl.pallas_call(middle_kernel, out_shape=(dq_shape, part_shape, part_shape...  6.35 us
    pallas_call x1, Pallas kernels, body(): pl.pallas_call(last_kernel, out_shape=(jax.ShapeDtypeStruct((R, 2 * QR +...  5.87 us
    pallas_call x1, Pallas kernels, prep(): pl.pallas_call(prep_kernel, out_shape=(shape, shape), in_specs=[SMEM, SME...  5.54 us
    ppermute x1, starting transfers between devices, body(): recv = lax.ppermute(send, 'core', [(0, 1), (1, 0)])  5.22 us
  transfers between devices with their start and end apart: 11, of which 5 were waited for; matrix products, arithmetic and copies ran while one was open for 0% of the time, Pallas kernels for 23%

profile of v5, /device:TPU:1, one launch (start us, length us, event | category | flops | bytes accessed | tf_op | source)
XLA Modules:
  0.0 96.6 jit_solution(14510764986007069286)
XLA Ops:
  0.6 1.5 %shards.1.order_by = bf16[256,512]{1,0:T(8,128)(2,1)} custom-call(s32[1]{0:T(128)} %bitcast.core.core_ref, bf16[16,512]{1,0:T(8,128)(2,1)} %k.1, bf16[16,512]{1,0:T(8,128)(2,1)} %v.1), custom_call_target="tpu_custom_call" | custom-call | tf_op jit(solution)/shard_map/shards/pallas_call | solution.py:268
  2.1 12.0 %all-to-all-start = ((bf16[16,16,512]{2,1,0:T(8,128)(2,1)}), bf16[16,16,512]{2,1,0:T(8,128)(2,1)S(1)}, u32[]{:S(2)}, u32[]{:S(2)}) async-start(bf16[16,16,512]{2,1,0:T(8,128)(2,1)} %bitcast.21), calls=%async_computation | async-start | bytes 524288 | tf_op jit(solution)/shard_map/all_to_all | solution.py:304
  14.7 5.5 %prep.1 = (bf16[2,2352,128]{2,1,0:T(8,128)(2,1)}, bf16[2,2352,128]{2,1,0:T(8,128)(2,1)}) custom-call(s32[1]{0:T(128)} %bitcast.core.core_ref, s32[1]{0:T(128)S(6)} %copy.28.length_ref, bf16[128,4096]{1,0:T(8,128)(2,1)} %bitcast.23, bf16[128,4096]{1,0:T(8,128)(2,1)} %bitcast.24, bf16[128,4096]{1,0:T(8,128)(2,1)} %bitcast.25, bf16[128,512]{1,0:T(8,128)(2,1)} %bitcast.26, ...), custom_call_target="tpu_custom_call" | custom-call | flops 10000000 | bytes 8388608 | tf_op jit(solution)/shard_map/prep/pallas_call | solution.py:99
  20.3 0.0 copy-start.2
  20.3 2.1 %all-to-all-done = bf16[16,16,512]{2,1,0:T(8,128)(2,1)S(1)} async-done(((bf16[16,16,512]{2,1,0:T(8,128)(2,1)}), bf16[16,16,512]{2,1,0:T(8,128)(2,1)S(1)}, u32[]{:S(2)}, u32[]{:S(2)}) %all-to-all-start) | async-done | bytes 262176 | tf_op jit(solution)/shard_map/all_to_all | solution.py:304
  22.4 0.0 copy-start
  22.4 0.7 copy-done
  23.1 5.2 %collective-permute-start = (bf16[2,2352,128]{2,1,0:T(8,128)(2,1)}, bf16[2,2352,128]{2,1,0:T(8,128)(2,1)S(1)}, u32[]{:S(2)}, u32[]{:S(2)}) collective-permute-start(bf16[2,2352,128]{2,1,0:T(8,128)(2,1)} %get-tuple-element.28), channel_id=1, source_target_pairs={{0,64},{64,0},{1,65},{65,1},{2,66},{66,2},{3,67},{67,3},{4,68},{68... | collective-permute-start | bytes 3612680 | tf_op jit(solution)/shard_map/ppermute | solution.py:327
  28.3 4.7 %collective-permute-start.3 = (bf16[256,512]{1,0:T(8,128)(2,1)}, bf16[256,512]{1,0:T(8,128)(2,1)S(1)}, u32[]{:S(2)}, u32[]{:S(2)}) collective-permute-start(bf16[256,512]{1,0:T(8,128)(2,1)} %get-tuple-element.29.kv), channel_id=1, source_target_pairs={{0,32},{16,48},{32,0},{48,16},{1,33},{17,49},{33,1},{49,17},{2,34}... | collective-permute-start | bytes 786440 | tf_op jit(solution)/shard_map/ppermute | solution.py:330
  33.0 2.8 %collective-permute-start.2 = (bf16[256,512]{1,0:T(8,128)(2,1)}, bf16[256,512]{1,0:T(8,128)(2,1)S(1)}, u32[]{:S(2)}, u32[]{:S(2)}) collective-permute-start(bf16[256,512]{1,0:T(8,128)(2,1)} %get-tuple-element.29.kv), channel_id=1, source_target_pairs={{0,48},{16,32},{32,16},{48,0},{1,49},{17,33},{33,17},{49,1},{2,50}... | collective-permute-start | bytes 786440 | tf_op jit(solution)/shard_map/ppermute | solution.py:330
  35.8 1.9 %collective-permute-start.1 = (bf16[256,512]{1,0:T(8,128)(2,1)}, bf16[256,512]{1,0:T(8,128)(2,1)S(1)}, u32[]{:S(2)}, u32[]{:S(2)}) collective-permute-start(bf16[256,512]{1,0:T(8,128)(2,1)} %get-tuple-element.29.kv), channel_id=1, source_target_pairs={{0,16},{16,0},{32,48},{48,32},{1,17},{17,1},{33,49},{49,33},{2,18}... | collective-permute-start | bytes 786440 | tf_op jit(solution)/shard_map/ppermute | solution.py:330
  37.7 2.2 %collective-permute-done.3.kv = bf16[256,512]{1,0:T(8,128)(2,1)S(1)} collective-permute-done((bf16[256,512]{1,0:T(8,128)(2,1)}, bf16[256,512]{1,0:T(8,128)(2,1)S(1)}, u32[]{:S(2)}, u32[]{:S(2)}) %collective-permute-start.3) | collective-permute-done | bytes 262176 | tf_op jit(solution)/shard_map/ppermute | solution.py:330
  39.9 0.0 collective-permute-done.recv
  39.9 0.0 copy-done.2
  39.9 3.0 %far_block.1 = (f32[2,2,1024,128]{3,2,1,0:T(8,128)S(1)}, bf16[256,512]{1,0:T(8,128)(2,1)S(1)}) custom-call(bf16[2,2352,128]{2,1,0:T(8,128)(2,1)S(1)} %copy-done.2, bf16[2,2352,128]{2,1,0:T(8,128)(2,1)S(1)} %collective-permute-done.recv, bf16[256,512]{1,0:T(8,128)(2,1)S(1)} %collective-permute-done.3.kv), custom_call_target="tpu_custom_call" | custom-call | flops 1342177280 | bytes 8388608 | tf_op jit(solution)/shard_map/far_block/pallas_call | solution.py:337
  42.9 4.7 %collective-permute-start.4 = (bf16[256,512]{1,0:T(8,128)(2,1)S(1)}, bf16[256,512]{1,0:T(8,128)(2,1)S(1)}, u32[]{:S(2)}, u32[]{:S(2)}) collective-permute-start(bf16[256,512]{1,0:T(8,128)(2,1)S(1)} %get-tuple-element.32), channel_id=1, source_target_pairs={{0,32},{16,48},{32,0},{48,16},{1,33},{17,49},{33,1},{49,17},{2,34}... | collective-permute-start | bytes 786440 | tf_op jit(solution)/shard_map/ppermute | solution.py:330
  47.6 0.0 collective-permute-done.2.kv_b
  47.6 0.0 collective-permute-done.1.kv_a
  47.6 0.0 copy-start.1
  47.6 6.4 %near_blocks.1 = (f32[2,2,1024,128]{3,2,1,0:T(8,128)S(1)}, bf16[256,512]{1,0:T(8,128)(2,1)S(1)}, bf16[256,512]{1,0:T(8,128)(2,1)S(1)}) custom-call(bf16[2,2352,128]{2,1,0:T(8,128)(2,1)S(1)} %copy-done.2, bf16[2,2352,128]{2,1,0:T(8,128)(2,1)S(1)} %collective-permute-done.recv, ...), custom_call_target="tpu_custom_call", output_to_operand_aliasing={{0}: (4, {})} | custom-call | flops 2684354560 | bytes 8388608 | tf_op jit(solution)/shard_map/near_blocks/pallas_call | solution.py:347
  54.0 2.8 %collective-permute-start.5 = (bf16[256,512]{1,0:T(8,128)(2,1)S(1)}, bf16[256,512]{1,0:T(8,128)(2,1)S(1)}, u32[]{:S(2)}, u32[]{:S(2)}) collective-permute-start(bf16[256,512]{1,0:T(8,128)(2,1)S(1)} %get-tuple-element.34), channel_id=1, source_target_pairs={{0,48},{16,32},{32,16},{48,0},{1,49},{17,33},{33,17},{49,1},{2,50}... | collective-permute-start | bytes 786440 | tf_op jit(solution)/shard_map/ppermute | solution.py:330
  56.8 2.1 %collective-permute-start.6 = (bf16[256,512]{1,0:T(8,128)(2,1)S(1)}, bf16[256,512]{1,0:T(8,128)(2,1)S(1)}, u32[]{:S(2)}, u32[]{:S(2)}) collective-permute-start(bf16[256,512]{1,0:T(8,128)(2,1)S(1)} %get-tuple-element.35), channel_id=1, source_target_pairs={{0,16},{16,0},{32,48},{48,32},{1,17},{17,1},{33,49},{49,33},{2,18}... | collective-permute-start | bytes 786440 | tf_op jit(solution)/shard_map/ppermute | solution.py:330
  58.9 0.0 collective-permute-done.4.order_by.b
  58.9 0.0 copy-done.1
  58.9 5.9 %own_block_and_own_keys.1 = (bf16[128,2560]{1,0:T(8,128)(2,1)S(1)}, f32[256,512]{1,0:T(8,128)S(1)}, bf16[128,4096]{1,0:T(8,128)(2,1)}, bf16[128,512]{1,0:T(8,128)(2,1)}, bf16[128,512]{1,0:T(8,128)(2,1)}) custom-call(s32[1]{0:T(128)} %bitcast.core.core_ref, bf16[2,2352,128]{2,1,0:T(8,128)(2,1)S(1)} %copy-done.2, ...), custom_call_target="tpu_custom_call" | custom-call | flops 2013265920 | bytes 8388608 | tf_op jit(solution)/shard_map/own_block_and_own_keys/pallas_call | solution.py:360
  64.8 0.0 collective-permute-done.5.c
  64.8 0.3 collective-permute-done.6.d
  65.0 0.8 sum_blocks.1
  65.9 3.7 %all-to-all-start.1 = ((bf16[16,16,512]{2,1,0:T(8,128)(2,1)}), bf16[16,16,512]{2,1,0:T(8,128)(2,1)S(1)}, u32[]{:S(2)}, u32[]{:S(2)}) async-start(bf16[16,16,512]{2,1,0:T(8,128)(2,1)} %bitcast.13), calls=%async_computation.1 | async-start | bytes 524288 | tf_op jit(solution)/shard_map/all_to_all | solution.py:395
  69.6 4.5 %collective-permute-start.7 = (bf16[128,2560]{1,0:T(8,128)(2,1)S(1)}, bf16[128,2560]{1,0:T(8,128)(2,1)S(1)}, u32[]{:S(2)}, u32[]{:S(2)}) collective-permute-start(bf16[128,2560]{1,0:T(8,128)(2,1)S(1)} %get-tuple-element.37), channel_id=1, source_target_pairs={{0,64},{64,0},{1,65},{65,1},{2,66},{66,2},{3,67},{67,3},{4,68},{68... | collective-permute-start | bytes 1966088 | tf_op jit(solution)/shard_map/ppermute | solution.py:394
  74.1 3.1 %all-to-all-done.1 = bf16[16,16,512]{2,1,0:T(8,128)(2,1)S(1)} async-done(((bf16[16,16,512]{2,1,0:T(8,128)(2,1)}), bf16[16,16,512]{2,1,0:T(8,128)(2,1)S(1)}, u32[]{:S(2)}, u32[]{:S(2)}) %all-to-all-start.1) | async-done | bytes 262176 | tf_op jit(solution)/shard_map/all_to_all | solution.py:395
  77.2 0.7 sum_copies.1
  77.9 10.0 %all-to-all-start.2 = ((bf16[8,16,512]{2,1,0:T(8,128)(2,1)}), bf16[8,16,512]{2,1,0:T(8,128)(2,1)S(1)}, u32[]{:S(2)}, u32[]{:S(2)}) async-start(bf16[8,16,512]{2,1,0:T(8,128)(2,1)} %bitcast.15), calls=%async_computation.2 | async-start | bytes 262144 | tf_op jit(solution)/shard_map/all_to_all | solution.py:399
  87.9 0.0 collective-permute-done.7.got
  87.9 0.8 join.1
  88.8 7.2 %all-to-all-done.2 = bf16[8,16,512]{2,1,0:T(8,128)(2,1)S(1)} async-done(((bf16[8,16,512]{2,1,0:T(8,128)(2,1)}), bf16[8,16,512]{2,1,0:T(8,128)(2,1)S(1)}, u32[]{:S(2)}, u32[]{:S(2)}) %all-to-all-start.2) | async-done | bytes 131104 | tf_op jit(solution)/shard_map/all_to_all | solution.py:399
  96.0 0.6 sum_samples.1
  (1 shorter events, 0.0 us)
Async XLA Ops:
  2.1 20.3 %all-to-all-start = ((bf16[16,16,512]{2,1,0:T(8,128)(2,1)}), bf16[16,16,512]{2,1,0:T(8,128)(2,1)S(1)}, u32[]{:S(2)}, u32[]{:S(2)}) async-start(bf16[16,16,512]{2,1,0:T(8,128)(2,1)} %bitcast.21), calls=%async_computation | async-start | bytes 524288 | tf_op jit(solution)/shard_map/all_to_all | solution.py:304
  20.3 19.6 %copy-start.2 = (bf16[2,2352,128]{2,1,0:T(8,128)(2,1)S(1)}, bf16[2,2352,128]{2,1,0:T(8,128)(2,1)}, u32[]{:S(2)}) copy-start(bf16[2,2352,128]{2,1,0:T(8,128)(2,1)} %get-tuple-element.26.mine) | copy-start | bytes 3612676
  22.4 0.7 copy-start
  23.1 16.8 %collective-permute-start = (bf16[2,2352,128]{2,1,0:T(8,128)(2,1)}, bf16[2,2352,128]{2,1,0:T(8,128)(2,1)S(1)}, u32[]{:S(2)}, u32[]{:S(2)}) collective-permute-start(bf16[2,2352,128]{2,1,0:T(8,128)(2,1)} %get-tuple-element.28), channel_id=1, source_target_pairs={{0,64},{64,0},{1,65},{65,1},{2,66},{66,2},{3,67},{67,3},{4,68},{68... | collective-permute-start | bytes 3612680 | tf_op jit(solution)/shard_map/ppermute | solution.py:327
  28.3 11.5 %collective-permute-start.3 = (bf16[256,512]{1,0:T(8,128)(2,1)}, bf16[256,512]{1,0:T(8,128)(2,1)S(1)}, u32[]{:S(2)}, u32[]{:S(2)}) collective-permute-start(bf16[256,512]{1,0:T(8,128)(2,1)} %get-tuple-element.29.kv), channel_id=1, source_target_pairs={{0,32},{16,48},{32,0},{48,16},{1,33},{17,49},{33,1},{49,17},{2,34}... | collective-permute-start | bytes 786440 | tf_op jit(solution)/shard_map/ppermute | solution.py:330
  33.0 14.6 %collective-permute-start.2 = (bf16[256,512]{1,0:T(8,128)(2,1)}, bf16[256,512]{1,0:T(8,128)(2,1)S(1)}, u32[]{:S(2)}, u32[]{:S(2)}) collective-permute-start(bf16[256,512]{1,0:T(8,128)(2,1)} %get-tuple-element.29.kv), channel_id=1, source_target_pairs={{0,48},{16,32},{32,16},{48,0},{1,49},{17,33},{33,17},{49,1},{2,50}... | collective-permute-start | bytes 786440 | tf_op jit(solution)/shard_map/ppermute | solution.py:330
  35.8 11.8 %collective-permute-start.1 = (bf16[256,512]{1,0:T(8,128)(2,1)}, bf16[256,512]{1,0:T(8,128)(2,1)S(1)}, u32[]{:S(2)}, u32[]{:S(2)}) collective-permute-start(bf16[256,512]{1,0:T(8,128)(2,1)} %get-tuple-element.29.kv), channel_id=1, source_target_pairs={{0,16},{16,0},{32,48},{48,32},{1,17},{17,1},{33,49},{49,33},{2,18}... | collective-permute-start | bytes 786440 | tf_op jit(solution)/shard_map/ppermute | solution.py:330
  42.9 16.0 %collective-permute-start.4 = (bf16[256,512]{1,0:T(8,128)(2,1)S(1)}, bf16[256,512]{1,0:T(8,128)(2,1)S(1)}, u32[]{:S(2)}, u32[]{:S(2)}) collective-permute-start(bf16[256,512]{1,0:T(8,128)(2,1)S(1)} %get-tuple-element.32), channel_id=1, source_target_pairs={{0,32},{16,48},{32,0},{48,16},{1,33},{17,49},{33,1},{49,17},{2,34}... | collective-permute-start | bytes 786440 | tf_op jit(solution)/shard_map/ppermute | solution.py:330
  47.6 11.3 %copy-start.1 = (bf16[256,512]{1,0:T(8,128)(2,1)S(1)}, bf16[256,512]{1,0:T(8,128)(2,1)}, u32[]{:S(2)}) copy-start(bf16[256,512]{1,0:T(8,128)(2,1)} %get-tuple-element.29.kv) | copy-start | bytes 786436
  54.0 10.8 %collective-permute-start.5 = (bf16[256,512]{1,0:T(8,128)(2,1)S(1)}, bf16[256,512]{1,0:T(8,128)(2,1)S(1)}, u32[]{:S(2)}, u32[]{:S(2)}) collective-permute-start(bf16[256,512]{1,0:T(8,128)(2,1)S(1)} %get-tuple-element.34), channel_id=1, source_target_pairs={{0,48},{16,32},{32,16},{48,0},{1,49},{17,33},{33,17},{49,1},{2,50}... | collective-permute-start | bytes 786440 | tf_op jit(solution)/shard_map/ppermute | solution.py:330
  56.8 8.3 %collective-permute-start.6 = (bf16[256,512]{1,0:T(8,128)(2,1)S(1)}, bf16[256,512]{1,0:T(8,128)(2,1)S(1)}, u32[]{:S(2)}, u32[]{:S(2)}) collective-permute-start(bf16[256,512]{1,0:T(8,128)(2,1)S(1)} %get-tuple-element.35), channel_id=1, source_target_pairs={{0,16},{16,0},{32,48},{48,32},{1,17},{17,1},{33,49},{49,33},{2,18}... | collective-permute-start | bytes 786440 | tf_op jit(solution)/shard_map/ppermute | solution.py:330
  65.9 11.3 %all-to-all-start.1 = ((bf16[16,16,512]{2,1,0:T(8,128)(2,1)}), bf16[16,16,512]{2,1,0:T(8,128)(2,1)S(1)}, u32[]{:S(2)}, u32[]{:S(2)}) async-start(bf16[16,16,512]{2,1,0:T(8,128)(2,1)} %bitcast.13), calls=%async_computation.1 | async-start | bytes 524288 | tf_op jit(solution)/shard_map/all_to_all | solution.py:395
  69.6 18.4 %collective-permute-start.7 = (bf16[128,2560]{1,0:T(8,128)(2,1)S(1)}, bf16[128,2560]{1,0:T(8,128)(2,1)S(1)}, u32[]{:S(2)}, u32[]{:S(2)}) collective-permute-start(bf16[128,2560]{1,0:T(8,128)(2,1)S(1)} %get-tuple-element.37), channel_id=1, source_target_pairs={{0,64},{64,0},{1,65},{65,1},{2,66},{66,2},{3,67},{67,3},{4,68},{68... | collective-permute-start | bytes 1966088 | tf_op jit(solution)/shard_map/ppermute | solution.py:394
  77.9 18.1 %all-to-all-start.2 = ((bf16[8,16,512]{2,1,0:T(8,128)(2,1)}), bf16[8,16,512]{2,1,0:T(8,128)(2,1)S(1)}, u32[]{:S(2)}, u32[]{:S(2)}) async-start(bf16[8,16,512]{2,1,0:T(8,128)(2,1)} %bitcast.15), calls=%async_computation.2 | async-start | bytes 262144 | tf_op jit(solution)/shard_map/all_to_all | solution.py:399
